TPU v7x, 512 devices: a whole 4x8x8 slice. The times are simulated.
512 devices in a mesh: tm: 4 (over z_lo), row: 16 (over y, core), head: 8 (over x, z_hi).
Axes of the slice: x: 4, y: 8, z: 8 (z_hi: 2, z_lo: 4; z = z_hi * 4 + z_lo), core: 2. Of those that a mesh axis runs over, the one named last changes fastest.
Arguments:
- queries: bfloat16 [8, 64, 16, 5120], P('tm', 'row', None, 'head'), may hold values from -24 to 24
- key_states: bfloat16 [8, 64, 16, 5120], P('tm', 'row', None, 'head'), may hold values from -24 to 24
- value_states: bfloat16 [8, 64, 16, 5120], P('tm', 'row', None, 'head'), may hold values from -6 to 6
- grad_output: bfloat16 [8, 64, 16, 5120], P('tm', 'row', None, 'head'), may hold values from -6 to 6
- window_mask: int32 [4, 32, 1, 27], P('tm', 'row'), may hold values from 0 to 1, as said below
- row_valid: int32 [8, 64], replicated, may hold values 0 or 1
Outputs:
- output: bfloat16 [8, 64, 16, 5120], P('tm', 'row', None, 'head')
- grad_queries: bfloat16 [8, 64, 16, 5120], P('tm', 'row', None, 'head')
- grad_keys: bfloat16 [8, 64, 16, 5120], P('tm', 'row', None, 'head')
- grad_values: bfloat16 [8, 64, 16, 5120], P('tm', 'row', None, 'head')
Inputs may be any that keep to these rules, and one draw needn't show every extreme that they name: `window_mask`: entry 13 (the tile itself) is 1 for every tile; entries whose tile lies outside the grid are 0; the mask is symmetric: tile A keeps tile B exactly when B keeps A at the opposite offset.
All inputs are finite; a program needn't handle non-finite values.
Results may differ from a plain program's by a relative error of at most 0.012.
Values may be sent and summed in bfloat16 or wider, within the bound.
No kernel may reach another device: no remote copies, remote signals or barrier semaphores. Data moves between devices by JAX's collectives and lax.ppermute only.
A program may use at most 64 MiB of HBM per device.

v0:
```python
import jax
import jax.numpy as jnp
from jax import lax
from jax.sharding import PartitionSpec as P

HD = 128
TF = 2
TR = 2
TC = 16


far_below = -1e30


def extended(block, sides, width):
    for axis, dim in sides:
        count = lax.axis_size(axis)
        forward = [(i, i + 1) for i in range(count - 1)]
        backward = [(target, source) for source, target in forward]
        low = lax.ppermute(
            lax.slice_in_dim(block, block.shape[dim] - width, None, axis=dim), axis, forward
        )
        high = lax.ppermute(lax.slice_in_dim(block, 0, width, axis=dim), axis, backward)
        block = jnp.concatenate([low, block, high], axis=dim)
    return block


def shifted(value, axis, steps):
    count = lax.axis_size(axis)
    leading, last = (max(0, -steps), min(count, count - steps))
    return lax.ppermute(value, axis, [(source, source + steps) for source in range(leading, last)])


def contract_last(left, right):
    return lax.dot_general(
        left, right, (((1,), (1,)), ((), ())), preferred_element_type=jnp.float32
    )


def contract_first(left, right):
    return lax.dot_general(
        left, right, (((0,), (0,)), ((), ())), preferred_element_type=jnp.float32
    )


def head_part(flat, head_index):
    return lax.dynamic_slice_in_dim(flat, head_index * HD, HD, 1)


def merge_heads(stacked, full_shape):
    return jnp.transpose(stacked, (1, 0, 2)).reshape(full_shape)


def allowed_pairs(window_mask, row_valid, rows_here):
    row_tiles = window_mask.shape[1]
    col_tiles = window_mask.shape[2]
    offsets = jnp.arange(27, dtype=jnp.int32)
    frame_step = offsets // 9
    row_step = offsets // 3 % 3 - 1
    col_step = offsets % 3 - 1
    tile_rows = jnp.arange(row_tiles, dtype=jnp.int32)
    tile_cols = jnp.arange(col_tiles, dtype=jnp.int32)
    near_frames = jnp.arange(3, dtype=jnp.int32)
    near_rows = jnp.arange(row_tiles + 2, dtype=jnp.int32)
    match_frame = near_frames[None, :] == frame_step[:, None]
    match_row = near_rows[None, None, :] == tile_rows[None, :, None] + row_step[:, None, None] + 1
    match_col = tile_cols[None, None, :] == tile_cols[None, :, None] + col_step[:, None, None]
    selector = (
        match_frame[:, None, None, :, None, None]
        & match_row[:, :, None, None, :, None]
        & match_col[:, None, :, None, None, :]
    )
    tile_keep = jnp.einsum(
        "abo,oabxyz->abxyz", window_mask[0].astype(jnp.float32), selector.astype(jnp.float32)
    )
    grown = jnp.repeat(tile_keep, TR, axis=0)
    grown = jnp.repeat(grown, TC, axis=1)
    grown = jnp.repeat(grown, TF, axis=2)
    grown = jnp.repeat(grown, TR, axis=3)
    grown = jnp.repeat(grown, TC, axis=4)
    padded_valid = jnp.pad(row_valid, ((TF, TF), (TR, TR)))
    beside_all = (
        lax.dynamic_slice(
            padded_valid,
            (lax.axis_index("tm") * TF, lax.axis_index("row") * rows_here),
            (3 * TF, rows_here + 2 * TR),
        )
        > 0
    )
    own = beside_all[TF : 2 * TF, TR : TR + rows_here]
    col_count = col_tiles * TC
    token_count = TF * rows_here * col_count
    pairs = (
        (grown[None] > 0.5)
        & own[:, :, None, None, None, None]
        & beside_all[None, None, None, :, :, None]
    )
    live_rows = jnp.broadcast_to(own[:, :, None], (TF, rows_here, col_count)).reshape(token_count)
    return (pairs.reshape(token_count, -1), live_rows)


def attend_head(query_head, key_head, value_head, grad_head, allowed, live_rows):
    score_scale = HD ** (-0.5)
    scores = contract_last(query_head, key_head) * score_scale
    row_max = jnp.max(jnp.where(allowed, scores, far_below), axis=1, keepdims=True)
    unnormed = jnp.exp(jnp.where(allowed, scores - row_max, -jnp.inf))
    denominator = (
        jnp.sum(unnormed, axis=1, keepdims=True) + (1.0 - live_rows.astype(jnp.float32))[:, None]
    )
    attended = (
        jnp.dot(unnormed.astype(jnp.bfloat16), value_head, preferred_element_type=jnp.float32)
        / denominator
    )
    head_output = attended.astype(jnp.bfloat16)
    log_total = jnp.where(live_rows[:, None], row_max + jnp.log(denominator), 0.0)
    row_dot = jnp.sum(head_output.astype(jnp.float32) * grad_head.astype(jnp.float32), axis=1)
    weights = jnp.exp(jnp.where(allowed, scores - log_total, -jnp.inf))
    grad_probs = contract_last(grad_head, value_head)
    grad_scores = (weights * (grad_probs - row_dot[:, None])).astype(jnp.bfloat16)
    grad_query = (
        jnp.dot(grad_scores, key_head, preferred_element_type=jnp.float32) * score_scale
    ).astype(jnp.bfloat16)
    return (head_output, log_total[:, 0], row_dot, weights, grad_scores, grad_query)


def shards(queries, key_states, value_states, grad_output, window_mask, row_valid):
    frames, rows_here, col_count, features = queries.shape
    head_count = features // HD
    token_count = frames * rows_here * col_count
    score_scale = HD ** (-0.5)
    allowed, live_rows = allowed_pairs(window_mask, row_valid, rows_here)
    key_value = jnp.stack([key_states, value_states])
    region = extended(key_value, (("tm", 1), ("row", 2)), TF)
    key_flat = region[0].reshape(-1, features)
    value_flat = region[1].reshape(-1, features)
    query_flat = queries.reshape(token_count, features)
    grad_flat = grad_output.reshape(token_count, features)
    head_ids = jnp.arange(head_count, dtype=jnp.int32)

    def push_head(head_index):
        query_head = head_part(query_flat, head_index)
        grad_head = head_part(grad_flat, head_index)
        head_output, log_total, row_dot, weights, grad_scores, grad_query = attend_head(
            query_head,
            head_part(key_flat, head_index),
            head_part(value_flat, head_index),
            grad_head,
            allowed,
            live_rows,
        )
        grad_key = contract_first(grad_scores, query_head) * score_scale
        grad_value = contract_first(weights.astype(jnp.bfloat16), grad_head)
        return (head_output, grad_query, grad_key, grad_value)

    outputs, query_heads, key_heads, value_heads = lax.map(push_head, head_ids)
    partials = jnp.transpose(jnp.stack([key_heads, value_heads]), (0, 2, 1, 3)).reshape(
        region.shape
    )
    from_above = shifted(partials[:, :, :TR].astype(jnp.bfloat16), "row", -1).astype(jnp.float32)
    from_below = shifted(partials[:, :, rows_here + TR :].astype(jnp.bfloat16), "row", 1).astype(
        jnp.float32
    )
    middle = partials[:, :, TR : TR + rows_here]
    middle = middle.at[:, :, rows_here - TR :].add(from_above)
    middle = middle.at[:, :, :TR].add(from_below)
    from_later = shifted(middle[:, :TF].astype(jnp.bfloat16), "tm", -1).astype(jnp.float32)
    from_earlier = shifted(middle[:, 2 * TF :].astype(jnp.bfloat16), "tm", 1).astype(jnp.float32)
    summed = middle[:, TF : 2 * TF] + from_later + from_earlier
    grad_keys = summed[0].astype(jnp.bfloat16)
    grad_values = summed[1].astype(jnp.bfloat16)
    output = merge_heads(outputs, queries.shape)
    grad_queries = merge_heads(query_heads, queries.shape)
    return (output, grad_queries, grad_keys, grad_values)


def solution(mesh):
    placed = (
        P("tm", "row", None, "head"),
        P("tm", "row", None, "head"),
        P("tm", "row", None, "head"),
        P("tm", "row", None, "head"),
        P("tm", "row", None, None),
        P(),
    )
    return jax.shard_map(
        shards,
        mesh=mesh,
        in_specs=placed,
        out_specs=(
            P("tm", "row", None, "head"),
            P("tm", "row", None, "head"),
            P("tm", "row", None, "head"),
            P("tm", "row", None, "head"),
        ),
        check_vma=False,
    )
```

profile of v0, /device:TPU:486, one launch (start us, length us, event | category | flops | bytes accessed | tf_op | source)
XLA Modules:
  0.0 124.7 jit_solution(7965430205111649710)
XLA Ops:
  1.7 2.5 %collective-permute-start.1 = (bf16[2,2,4,16,640]{4,3,2,1,0:T(8,128)(2,1)S(1)}, bf16[2,2,4,16,640]{4,3,2,1,0:T(8,128)(2,1)S(1)}, u32[]{:S(2)}, u32[]{:S(2)}) collective-permute-start(bf16[2,2,4,16,640]{4,3,2,1,0:T(8,128)(2,1)S(1)} %pad_maximum_fusion.2), channel_id=1, source_target_pairs={{128,0},{256,128},{384,256},{129,1},{257,129},{385,257},{130,2},{2... | collective-permute-start | bytes 983048 | tf_op jit(solution)/shard_map/ppermute | solution.py:23
  5.9 5.1 %collective-permute-done.1 = bf16[2,2,4,16,640]{4,3,2,1,0:T(8,128)(2,1)S(1)} collective-permute-done((bf16[2,2,4,16,640]{4,3,2,1,0:T(8,128)(2,1)S(1)}, bf16[2,2,4,16,640]{4,3,2,1,0:T(8,128)(2,1)S(1)}, u32[]{:S(2)}, u32[]{:S(2)}) %collective-permute-start.1) | collective-permute-done | bytes 327712 | tf_op jit(solution)/shard_map/ppermute | solution.py:23
  11.1 4.1 %collective-permute-done = bf16[2,2,4,16,640]{4,3,2,1,0:T(8,128)(2,1)S(1)} collective-permute-done((bf16[2,2,4,16,640]{4,3,2,1,0:T(8,128)(2,1)S(1)}, bf16[2,2,4,16,640]{4,3,2,1,0:T(8,128)(2,1)S(1)}, u32[]{:S(2)}, u32[]{:S(2)}) %collective-permute-start) | collective-permute-done | bytes 327712 | tf_op jit(solution)/shard_map/ppermute | solution.py:20
  16.5 1.9 %collective-permute-start.2 = (bf16[2,6,2,16,640]{4,3,2,1,0:T(8,128)(2,1)S(1)}, bf16[2,6,2,16,640]{4,3,2,1,0:T(8,128)(2,1)S(1)}, u32[]{:S(2)}, u32[]{:S(2)}) collective-permute-start(bf16[2,6,2,16,640]{4,3,2,1,0:T(8,128)(2,1)S(1)} %get-tuple-element.243), channel_id=1, source_target_pairs={{0,8},{8,16},{16,24},{24,32},{32,40},{40,48},{48,56},{56,64},{64,7... | collective-permute-start | bytes 1474568 | tf_op jit(solution)/shard_map/ppermute | solution.py:20
  18.4 4.9 %collective-permute-start.3 = (bf16[2,6,2,16,640]{4,3,2,1,0:T(8,128)(2,1)S(1)}, bf16[2,6,2,16,640]{4,3,2,1,0:T(8,128)(2,1)S(1)}, u32[]{:S(2)}, u32[]{:S(2)}) collective-permute-start(bf16[2,6,2,16,640]{4,3,2,1,0:T(8,128)(2,1)S(1)} %get-tuple-element.244), channel_id=1, source_target_pairs={{8,0},{16,8},{24,16},{32,24},{40,32},{48,40},{56,48},{64,56},{72,6... | collective-permute-start | bytes 1474568 | tf_op jit(solution)/shard_map/ppermute | solution.py:23
  24.2 3.6 %collective-permute-done.2 = bf16[2,6,2,16,640]{4,3,2,1,0:T(8,128)(2,1)S(1)} collective-permute-done((bf16[2,6,2,16,640]{4,3,2,1,0:T(8,128)(2,1)S(1)}, bf16[2,6,2,16,640]{4,3,2,1,0:T(8,128)(2,1)S(1)}, u32[]{:S(2)}, u32[]{:S(2)}) %collective-permute-start.2) | collective-permute-done | bytes 491552 | tf_op jit(solution)/shard_map/ppermute | solution.py:20
  27.8 1.8 %collective-permute-done.3 = bf16[2,6,2,16,640]{4,3,2,1,0:T(8,128)(2,1)S(1)} collective-permute-done((bf16[2,6,2,16,640]{4,3,2,1,0:T(8,128)(2,1)S(1)}, bf16[2,6,2,16,640]{4,3,2,1,0:T(8,128)(2,1)S(1)}, u32[]{:S(2)}, u32[]{:S(2)}) %collective-permute-start.3) | collective-permute-done | bytes 491552 | tf_op jit(solution)/shard_map/ppermute | solution.py:23
  30.1 48.5 %while.20 = (s32[]{:T(128)}, bf16[5,128,128]{1,2,0:T(8,128)(2,1)S(1)}, bf16[5,128,128]{2,1,0:T(8,128)(2,1)}, f32[5,768,128]{2,1,0:T(8,128)}, f32[5,768,128]{2,1,...) while((s32[]{:T(128)}, ...), condition=%wide.region_4.5_spmd.clone.clone, body=%wide.region_0.4_spmd.clone.clone.sunk | while | flops 153878784 | bytes 5356243 | solution.py:155
  32.7 1.3 %and.291 = pred[128,768]{1,0:T(32,128)(4,1)S(1)} reshape(pred[2,4,16,6,8,16]{5,4,3,2,1,0:T(8,128)(4,1)S(1)} %and.290) | data formatting | bytes 196608 | tf_op jit(solution)/shard_map/and | solution.py:94
  38.1 1.7 %fusion.80 = f32[5,768,128]{2,1,0:T(8,128)} fusion(f32[5,768,128]{2,1,0:T(8,128)} %get-tuple-element.367, s32[]{:T(128)S(6)} %copy.43, bf16[128,768]{1,0:T(8,128)(2,1)S(1)} %fusion.78, bf16[128,640]{1,0:T(8,128)(2,1)} %get-tuple-element.388, s32[]{:T(128)S(6)} %select_n.128), kind=kOutput, calls=%fused_computation.7.clone.1 | convolution fusion | flops 25264128 | bytes 622600 | tf_op jit(solution)/shard_map/while/body/eval_jaxpr/dot_general | solution.py:41
  47.8 1.7 %fusion.80 = f32[5,768,128]{2,1,0:T(8,128)} fusion(f32[5,768,128]{2,1,0:T(8,128)} %get-tuple-element.367, s32[]{:T(128)S(6)} %copy.43, bf16[128,768]{1,0:T(8,128)(2,1)S(1)} %fusion.78, bf16[128,640]{1,0:T(8,128)(2,1)} %get-tuple-element.388, s32[]{:T(128)S(6)} %select_n.128), kind=kOutput, calls=%fused_computation.7.clone.1 | convolution fusion | flops 25264128 | bytes 622600 | tf_op jit(solution)/shard_map/while/body/eval_jaxpr/dot_general | solution.py:41
  57.5 1.7 %fusion.80 = f32[5,768,128]{2,1,0:T(8,128)} fusion(f32[5,768,128]{2,1,0:T(8,128)} %get-tuple-element.367, s32[]{:T(128)S(6)} %copy.43, bf16[128,768]{1,0:T(8,128)(2,1)S(1)} %fusion.78, bf16[128,640]{1,0:T(8,128)(2,1)} %get-tuple-element.388, s32[]{:T(128)S(6)} %select_n.128), kind=kOutput, calls=%fused_computation.7.clone.1 | convolution fusion | flops 25264128 | bytes 622600 | tf_op jit(solution)/shard_map/while/body/eval_jaxpr/dot_general | solution.py:41
  67.2 1.7 %fusion.80 = f32[5,768,128]{2,1,0:T(8,128)} fusion(f32[5,768,128]{2,1,0:T(8,128)} %get-tuple-element.367, s32[]{:T(128)S(6)} %copy.43, bf16[128,768]{1,0:T(8,128)(2,1)S(1)} %fusion.78, bf16[128,640]{1,0:T(8,128)(2,1)} %get-tuple-element.388, s32[]{:T(128)S(6)} %select_n.128), kind=kOutput, calls=%fused_computation.7.clone.1 | convolution fusion | flops 25264128 | bytes 622600 | tf_op jit(solution)/shard_map/while/body/eval_jaxpr/dot_general | solution.py:41
  76.8 1.7 %fusion.80 = f32[5,768,128]{2,1,0:T(8,128)} fusion(f32[5,768,128]{2,1,0:T(8,128)} %get-tuple-element.367, s32[]{:T(128)S(6)} %copy.43, bf16[128,768]{1,0:T(8,128)(2,1)S(1)} %fusion.78, bf16[128,640]{1,0:T(8,128)(2,1)} %get-tuple-element.388, s32[]{:T(128)S(6)} %select_n.128), kind=kOutput, calls=%fused_computation.7.clone.1 | convolution fusion | flops 25264128 | bytes 622600 | tf_op jit(solution)/shard_map/while/body/eval_jaxpr/dot_general | solution.py:41
  78.6 2.5 %maximum_bitcast_fusion = f32[2,768,5,128]{3,1,2,0:T(8,128)S(1)} fusion(f32[1,5,768,128]{3,2,1,0:T(8,128)} %bitcast.68, f32[1,5,768,128]{3,2,1,0:T(8,128)} %bitcast.69), kind=kLoop, calls=%fused_computation.47 | loop fusion | flops 983040 | bytes 7864320 | tf_op jit(solution)/shard_map/transpose | solution.py:156
  81.1 5.0 %copy.24 = f32[2,768,5,128]{3,2,1,0:T(8,128)} copy(f32[2,768,5,128]{3,1,2,0:T(8,128)S(1)} %maximum_bitcast_fusion) | data formatting | bytes 7864320 | tf_op jit(solution)/shard_map/transpose | solution.py:156
  86.1 6.6 %reshape.277 = f32[2,6,8,16,640]{4,3,2,1,0:T(8,128)} reshape(f32[2,768,5,128]{3,2,1,0:T(8,128)} %copy.24) | data formatting | bytes 7864320 | tf_op jit(solution)/shard_map/reshape | solution.py:156
  92.7 2.4 %convert.12 = bf16[2,6,8,16,640]{4,3,2,1,0:T(8,128)(2,1)S(1)} convert(f32[2,6,8,16,640]{4,3,2,1,0:T(8,128)} %reshape.277) | non-fusion elementwise | flops 983040 | bytes 5898240 | tf_op jit(solution)/shard_map/convert.5
  95.2 5.3 %collective-permute-start.4 = (bf16[2,6,2,16,640]{4,3,2,1,0:T(8,128)(2,1)S(1)}, bf16[2,6,2,16,640]{4,3,2,1,0:T(8,128)(2,1)S(1)}, u32[]{:S(2)}, u32[]{:S(2)}) collective-permute-start(bf16[2,6,2,16,640]{4,3,2,1,0:T(8,128)(2,1)S(1)} %get-tuple-element.238), channel_id=1, source_target_pairs={{8,0},{16,8},{24,16},{32,24},{40,32},{48,40},{56,48},{64,56},{72,6... | collective-permute-start | bytes 1474568 | tf_op jit(solution)/shard_map/ppermute | solution.py:31
  100.5 2.1 %collective-permute-start.5 = (bf16[2,6,2,16,640]{4,3,2,1,0:T(8,128)(2,1)S(1)}, bf16[2,6,2,16,640]{4,3,2,1,0:T(8,128)(2,1)S(1)}, u32[]{:S(2)}, u32[]{:S(2)}) collective-permute-start(bf16[2,6,2,16,640]{4,3,2,1,0:T(8,128)(2,1)S(1)} %get-tuple-element.237), channel_id=1, source_target_pairs={{0,8},{8,16},{16,24},{24,32},{32,40},{40,48},{48,56},{56,64},{64,7... | collective-permute-start | bytes 1474568 | tf_op jit(solution)/shard_map/ppermute | solution.py:31
  102.6 4.3 %collective-permute-done.4 = bf16[2,6,2,16,640]{4,3,2,1,0:T(8,128)(2,1)S(1)} collective-permute-done((bf16[2,6,2,16,640]{4,3,2,1,0:T(8,128)(2,1)S(1)}, bf16[2,6,2,16,640]{4,3,2,1,0:T(8,128)(2,1)S(1)}, u32[]{:S(2)}, u32[]{:S(2)}) %collective-permute-start.4) | collective-permute-done | bytes 491552 | tf_op jit(solution)/shard_map/ppermute | solution.py:31
  106.9 5.1 %collective-permute-done.5 = bf16[2,6,2,16,640]{4,3,2,1,0:T(8,128)(2,1)S(1)} collective-permute-done((bf16[2,6,2,16,640]{4,3,2,1,0:T(8,128)(2,1)S(1)}, bf16[2,6,2,16,640]{4,3,2,1,0:T(8,128)(2,1)S(1)}, u32[]{:S(2)}, u32[]{:S(2)}) %collective-permute-start.5) | collective-permute-done | bytes 491552 | tf_op jit(solution)/shard_map/ppermute | solution.py:31
  112.4 2.5 %collective-permute-start.6 = (bf16[2,2,4,16,640]{4,3,2,1,0:T(8,128)(2,1)S(1)}, bf16[2,2,4,16,640]{4,3,2,1,0:T(8,128)(2,1)S(1)}, u32[]{:S(2)}, u32[]{:S(2)}) collective-permute-start(bf16[2,2,4,16,640]{4,3,2,1,0:T(8,128)(2,1)S(1)} %get-tuple-element.241), channel_id=1, source_target_pairs={{128,0},{256,128},{384,256},{129,1},{257,129},{385,257},{130,2},{2... | collective-permute-start | bytes 983048 | tf_op jit(solution)/shard_map/ppermute | solution.py:31
  120.1 3.8 %collective-permute-done.7 = bf16[2,2,4,16,640]{4,3,2,1,0:T(8,128)(2,1)S(1)} collective-permute-done((bf16[2,2,4,16,640]{4,3,2,1,0:T(8,128)(2,1)S(1)}, bf16[2,2,4,16,640]{4,3,2,1,0:T(8,128)(2,1)S(1)}, u32[]{:S(2)}, u32[]{:S(2)}) %collective-permute-start.7) | collective-permute-done | bytes 327712 | tf_op jit(solution)/shard_map/ppermute | solution.py:31
  (132 shorter events, 47.0 us)
Async XLA Ops:
  1.7 9.4 %collective-permute-start.1 = (bf16[2,2,4,16,640]{4,3,2,1,0:T(8,128)(2,1)S(1)}, bf16[2,2,4,16,640]{4,3,2,1,0:T(8,128)(2,1)S(1)}, u32[]{:S(2)}, u32[]{:S(2)}) collective-permute-start(bf16[2,2,4,16,640]{4,3,2,1,0:T(8,128)(2,1)S(1)} %pad_maximum_fusion.2), channel_id=1, source_target_pairs={{128,0},{256,128},{384,256},{129,1},{257,129},{385,257},{130,2},{2... | collective-permute-start | bytes 983048 | tf_op jit(solution)/shard_map/ppermute | solution.py:23
  4.2 11.1 %collective-permute-start = (bf16[2,2,4,16,640]{4,3,2,1,0:T(8,128)(2,1)S(1)}, bf16[2,2,4,16,640]{4,3,2,1,0:T(8,128)(2,1)S(1)}, u32[]{:S(2)}, u32[]{:S(2)}) collective-permute-start(bf16[2,2,4,16,640]{4,3,2,1,0:T(8,128)(2,1)S(1)} %pad_maximum_fusion.2), channel_id=1, source_target_pairs={{0,128},{128,256},{256,384},{1,129},{129,257},{257,385},{2,130},{1... | collective-permute-start | bytes 983048 | tf_op jit(solution)/shard_map/ppermute | solution.py:20
  5.9 17.4 %copy-start.4 = (s32[8,64]{1,0:T(8,128)S(1)}, s32[8,64]{1,0:T(8,128)}, u32[]{:S(2)}) copy-start(s32[8,64]{1,0:T(8,128)} %param.17) | copy-start | bytes 6148
  5.9 17.9 %copy-start.5 = (s32[1,2,1,27]{3,2,1,0:T(1,128)S(1)}, s32[1,2,1,27]{3,2,1,0:T(1,128)}, u32[]{:S(2)}) copy-start(s32[1,2,1,27]{3,2,1,0:T(1,128)} %param.16) | copy-start | bytes 652
  5.9 23.7 %copy-start.1 = (bf16[2,4,16,640]{3,2,1,0:T(8,128)(2,1)S(1)}, bf16[2,4,16,640]{3,2,1,0:T(8,128)(2,1)}, u32[]{:S(2)}) copy-start(bf16[2,4,16,640]{3,2,1,0:T(8,128)(2,1)} %param.14) | copy-start | bytes 491524
  5.9 23.6 %copy-start.2 = (bf16[2,4,16,640]{3,2,1,0:T(8,128)(2,1)S(1)}, bf16[2,4,16,640]{3,2,1,0:T(8,128)(2,1)}, u32[]{:S(2)}) copy-start(bf16[2,4,16,640]{3,2,1,0:T(8,128)(2,1)} %param.13) | copy-start | bytes 491524
  16.5 11.4 %collective-permute-start.2 = (bf16[2,6,2,16,640]{4,3,2,1,0:T(8,128)(2,1)S(1)}, bf16[2,6,2,16,640]{4,3,2,1,0:T(8,128)(2,1)S(1)}, u32[]{:S(2)}, u32[]{:S(2)}) collective-permute-start(bf16[2,6,2,16,640]{4,3,2,1,0:T(8,128)(2,1)S(1)} %get-tuple-element.243), channel_id=1, source_target_pairs={{0,8},{8,16},{16,24},{24,32},{32,40},{40,48},{48,56},{56,64},{64,7... | collective-permute-start | bytes 1474568 | tf_op jit(solution)/shard_map/ppermute | solution.py:20
  18.4 11.2 %collective-permute-start.3 = (bf16[2,6,2,16,640]{4,3,2,1,0:T(8,128)(2,1)S(1)}, bf16[2,6,2,16,640]{4,3,2,1,0:T(8,128)(2,1)S(1)}, u32[]{:S(2)}, u32[]{:S(2)}) collective-permute-start(bf16[2,6,2,16,640]{4,3,2,1,0:T(8,128)(2,1)S(1)} %get-tuple-element.244), channel_id=1, source_target_pairs={{8,0},{16,8},{24,16},{32,24},{40,32},{48,40},{56,48},{64,56},{72,6... | collective-permute-start | bytes 1474568 | tf_op jit(solution)/shard_map/ppermute | solution.py:23
  78.6 2.5 %copy-start.3 = (bf16[5,128,128]{1,2,0:T(8,128)(2,1)}, bf16[5,128,128]{1,2,0:T(8,128)(2,1)S(1)}, u32[]{:S(2)}) copy-start(bf16[5,128,128]{1,2,0:T(8,128)(2,1)S(1)} %get-tuple-element.98) | copy-start | bytes 491524
  95.1 11.7 %copy-start = (f32[2,6,8,16,640]{4,3,2,1,0:T(8,128)S(1)}, f32[2,6,8,16,640]{4,3,2,1,0:T(8,128)}, u32[]{:S(2)}) copy-start(f32[2,6,8,16,640]{4,3,2,1,0:T(8,128)} %reshape.277) | copy-start | bytes 11796484
  95.2 11.6 %collective-permute-start.4 = (bf16[2,6,2,16,640]{4,3,2,1,0:T(8,128)(2,1)S(1)}, bf16[2,6,2,16,640]{4,3,2,1,0:T(8,128)(2,1)S(1)}, u32[]{:S(2)}, u32[]{:S(2)}) collective-permute-start(bf16[2,6,2,16,640]{4,3,2,1,0:T(8,128)(2,1)S(1)} %get-tuple-element.238), channel_id=1, source_target_pairs={{8,0},{16,8},{24,16},{32,24},{40,32},{48,40},{56,48},{64,56},{72,6... | collective-permute-start | bytes 1474568 | tf_op jit(solution)/shard_map/ppermute | solution.py:31
  100.5 6.3 %slice-start = ((f32[2,6,8,16,640]{4,3,2,1,0:T(8,128)}), f32[2,6,4,16,640]{4,3,2,1,0:T(8,128)S(1)}, s32[]{:S(2)}) async-start(f32[2,6,8,16,640]{4,3,2,1,0:T(8,128)} %reshape.277), calls=%async_computation | async-start | bytes 3932160 | tf_op jit(solution)/shard_map/slice | solution.py:163
  100.5 11.5 %collective-permute-start.5 = (bf16[2,6,2,16,640]{4,3,2,1,0:T(8,128)(2,1)S(1)}, bf16[2,6,2,16,640]{4,3,2,1,0:T(8,128)(2,1)S(1)}, u32[]{:S(2)}, u32[]{:S(2)}) collective-permute-start(bf16[2,6,2,16,640]{4,3,2,1,0:T(8,128)(2,1)S(1)} %get-tuple-element.237), channel_id=1, source_target_pairs={{0,8},{8,16},{16,24},{24,32},{32,40},{40,48},{48,56},{56,64},{64,7... | collective-permute-start | bytes 1474568 | tf_op jit(solution)/shard_map/ppermute | solution.py:31
  112.4 7.7 %collective-permute-start.6 = (bf16[2,2,4,16,640]{4,3,2,1,0:T(8,128)(2,1)S(1)}, bf16[2,2,4,16,640]{4,3,2,1,0:T(8,128)(2,1)S(1)}, u32[]{:S(2)}, u32[]{:S(2)}) collective-permute-start(bf16[2,2,4,16,640]{4,3,2,1,0:T(8,128)(2,1)S(1)} %get-tuple-element.241), channel_id=1, source_target_pairs={{128,0},{256,128},{384,256},{129,1},{257,129},{385,257},{130,2},{2... | collective-permute-start | bytes 983048 | tf_op jit(solution)/shard_map/ppermute | solution.py:31
  114.9 9.0 %collective-permute-start.7 = (bf16[2,2,4,16,640]{4,3,2,1,0:T(8,128)(2,1)S(1)}, bf16[2,2,4,16,640]{4,3,2,1,0:T(8,128)(2,1)S(1)}, u32[]{:S(2)}, u32[]{:S(2)}) collective-permute-start(bf16[2,2,4,16,640]{4,3,2,1,0:T(8,128)(2,1)S(1)} %get-tuple-element.242), channel_id=1, source_target_pairs={{0,128},{128,256},{256,384},{1,129},{129,257},{257,385},{2,130},{1... | collective-permute-start | bytes 983048 | tf_op jit(solution)/shard_map/ppermute | solution.py:31
where the time goes:
time: 126 us; the launch traced here: 125 us
  local copies, waits for them, and re-layouts  33.4 us (27%)
  waiting for transfers between devices  27.7 us (22%)
  matrix products  27.4 us (22%)
  starting transfers between devices  21.6 us (17%)
  other arithmetic  10.1 us (8%)
  loops' own time  3.54 us (3%)
    dot_general x10, matrix products, contract_first(): lax.dot_general(left, right, (((0,), (0,)), ((), ())), preferred_element_...  14.4 us
    ppermute x4, waiting for transfers between devices, shifted(): lax.ppermute(value, axis, [(source, source + steps) for source in range(l...  13.1 us
    ppermute x4, starting transfers between devices, shifted(): lax.ppermute(value, axis, [(source, source + steps) for source in range(l...  11.1 us
    and x24, local copies, waits for them, and re-layouts, allowed_pairs(): (grown[None] > 0.5) & own[:, :, None, None, None, None]  9.06 us
    ppermute x2, waiting for transfers between devices, extended(): lax.ppermute(lax.slice_in_dim(block, block.shape[dim] - width, None, axis...  7.74 us
    ppermute x2, starting transfers between devices, extended(): lax.ppermute(lax.slice_in_dim(block, 0, width, axis=dim), axis, backward)  7.33 us
    ppermute x2, waiting for transfers between devices, extended(): lax.ppermute(lax.slice_in_dim(block, 0, width, axis=dim), axis, backward)  6.9 us
    dot_general x10, matrix products, contract_last(): lax.dot_general(left, right, (((1,), (1,)), ((), ())), preferred_element_...  6.67 us
  transfers between devices with their start and end apart: 8, of which 7 were waited for; matrix products, arithmetic and copies ran while one was open for 4% of the time, Pallas kernels for 0%

commit v1 on v0

v1 whole, which is shorter than its diff:
```python
import functools
import math

import jax
import jax.numpy as jnp
import numpy as np
from jax import lax
from jax.experimental import pallas as pl
from jax.experimental.pallas import tpu as pltpu
from jax.sharding import PartitionSpec as P

HD = 128
TF = 2
TR = 2
BAND = 64
HALF = BAND // 2
NEAR = 3 * TF * BAND
Q_AT = 2 * NEAR
G_AT = Q_AT + TF * BAND
MASK_AT = G_AT + TF * BAND
MASK_ROWS = 16
MESSAGE = MASK_AT + MASK_ROWS
OWN = TF * BAND
GROUPS = ((0, 5),)

SCALE = HD ** (-0.5)
SCALE_LOG2 = SCALE * math.log2(math.e)
FAR = 1e30


def contract(left, right, dims):
    return lax.dot_general(left, right, ((dims[:1], dims[1:]), ((), ())), preferred_element_type=jnp.float32)


SLOT_TILE = (2, 3, 1, 4)


def other_tile(slot, half):
    return ((1, 4), (1, 4), (0, 1), (4, 5))[slot][half]


def selectors():
    mask_pick = np.zeros((128, 2 * NEAR), np.float32)
    valid_pick = np.zeros((128, 4 * NEAR), np.float32)
    query_pick = np.zeros((4 * BAND, 128), np.float32)
    for lane in range(NEAR):
        frame, half, row = lane // BAND, lane % BAND // HALF, lane % HALF // 16
        valid_pick[frame * 12 + 4 + 2 * half + row, lane] = 1
        for part, slot in enumerate((0, 2, 3)):
            valid_pick[frame * 12 + 2 * other_tile(slot, half) + row, (part + 1) * NEAR + lane] = 1
        for slot in range(4):
            for part, tile in enumerate((2 + half, other_tile(slot, half))):
                step = tile - SLOT_TILE[slot]
                if abs(step) <= 1:
                    mask_pick[32 * slot + 9 * (frame // TF) + 3 * (step + 1) + 1, part * NEAR + lane] = 1
    for slot in range(4):
        for token in range(BAND):
            frame, row = token // HALF, token % HALF // 16
            query_pick[slot * BAND + token, (TF + frame) * 12 + 2 * SLOT_TILE[slot] + row] = 1
    return mask_pick, valid_pick, query_pick


def tiles(here, above, below, at, lanes):
    def piece(ref, frame, half):
        start = at + frame * BAND + half * HALF
        return ref[start : start + HALF, lanes]

    order = ((here, 0), (here, 1), (above, 1), (below, 0))
    return jnp.concatenate([piece(ref, frame, half) for ref, half in order for frame in range(TF)], axis=0)


def beside(above, below, at, lanes):
    parts = []
    for frame in range(3 * TF):
        start = at + frame * BAND
        parts += [above[start + HALF : start + BAND, lanes], below[start : start + HALF, lanes]]
    return jnp.concatenate(parts, axis=0)


def store_tiles(ref, value, lanes):
    for half in range(2):
        for frame in range(TF):
            start = frame * BAND + half * HALF
            source = half * BAND + frame * HALF
            ref[start : start + HALF, lanes] = value[source : source + HALF]


def attend(
    heads, here, above, below, valid, mask_pick, valid_pick, query_pick, output, grad_query, own_sum, low_sum, high_sum
):
    mask_lanes = slice(MASK_AT, MASK_AT + MASK_ROWS)
    slot = lax.broadcasted_iota(jnp.int32, (MASK_ROWS, 128), 0)
    masks = jnp.where(
        slot < 2,
        here[mask_lanes, :128].astype(jnp.float32),
        jnp.where(slot == 2, above[mask_lanes, :128].astype(jnp.float32), below[mask_lanes, :128].astype(jnp.float32)),
    ).astype(jnp.bfloat16)
    kept = contract(masks, mask_pick[...], (1, 0))
    live = contract(valid[...], valid_pick[...], (1, 0))
    query_live = contract(query_pick[...], valid[...], (1, 1))[:, :1]
    bias_own, bias_other = [], []
    for index in range(4):
        part = max(index - 1, 0) + 1
        keep_own = kept[index : index + 1, :NEAR] * live[:1, :NEAR]
        keep_other = kept[index : index + 1, NEAR:] * live[:1, part * NEAR : (part + 1) * NEAR]
        bias_own.append(jnp.broadcast_to((keep_own - 1.0) * FAR, (BAND, NEAR)))
        bias_other.append(jnp.broadcast_to((keep_other - 1.0) * FAR, (BAND, NEAR)))
    bias_own = jnp.concatenate(bias_own, axis=0)
    bias_other = jnp.concatenate(bias_other, axis=0)

    for head in range(heads):
        lanes = slice(head * HD, (head + 1) * HD)
        query = tiles(here, above, below, Q_AT, lanes)
        grad = tiles(here, above, below, G_AT, lanes)
        key_own, value_own = here[:NEAR, lanes], here[NEAR : 2 * NEAR, lanes]
        key_up, value_up = above[:NEAR, lanes], above[NEAR : 2 * NEAR, lanes]
        key_down, value_down = below[:NEAR, lanes], below[NEAR : 2 * NEAR, lanes]
        key_side, value_side = beside(above, below, 0, lanes), beside(above, below, NEAR, lanes)

        score_own = contract(query, key_own, (1, 1)) * SCALE_LOG2 + bias_own
        score_other = (
            jnp.concatenate(
                [
                    contract(query[:OWN], key_side, (1, 1)),
                    contract(query[OWN : OWN + BAND], key_up, (1, 1)),
                    contract(query[OWN + BAND :], key_down, (1, 1)),
                ],
                axis=0,
            )
            * SCALE_LOG2
            + bias_other
        )
        row_max = jnp.max(jnp.maximum(score_own, score_other), axis=1, keepdims=True)
        own = jnp.exp2(score_own - row_max)
        other = jnp.exp2(score_other - row_max)
        share = query_live / jnp.sum(own + other, axis=1, keepdims=True)
        own_bf, other_bf = own.astype(jnp.bfloat16), other.astype(jnp.bfloat16)
        attended = contract(own_bf, value_own, (1, 0)) + jnp.concatenate(
            [
                contract(other_bf[:OWN], value_side, (1, 0)),
                contract(other_bf[OWN : OWN + BAND], value_up, (1, 0)),
                contract(other_bf[OWN + BAND :], value_down, (1, 0)),
            ],
            axis=0,
        )
        result = (attended * share).astype(jnp.bfloat16)
        row_dot = jnp.sum(result.astype(jnp.float32) * grad.astype(jnp.float32), axis=1, keepdims=True)
        weight_own = own * share
        weight_side = other[:OWN] * share[:OWN]
        grad_score_own = (weight_own * (contract(grad, value_own, (1, 1)) - row_dot)).astype(jnp.bfloat16)
        grad_score_side = (weight_side * (contract(grad[:OWN], value_side, (1, 1)) - row_dot[:OWN])).astype(jnp.bfloat16)
        query_sum = contract(grad_score_own[:OWN], key_own, (1, 0)) + contract(grad_score_side, key_side, (1, 0))
        key_sum = contract(grad_score_own, query, (0, 0)) * SCALE
        value_sum = contract(weight_own.astype(jnp.bfloat16), grad, (0, 0))

        store_tiles(output, result, lanes)
        store_tiles(grad_query, (query_sum * SCALE).astype(jnp.bfloat16), lanes)
        for part, total in enumerate((key_sum, value_sum)):
            rows = slice(part * OWN, (part + 1) * OWN)
            low_sum[rows, lanes] = total[:OWN].astype(jnp.bfloat16)
            own_sum[rows, lanes] = total[OWN : 2 * OWN]
            high_sum[rows, lanes] = total[2 * OWN :].astype(jnp.bfloat16)


def shifted(value, axis, steps):
    count = lax.axis_size(axis)
    leading, last = (max(0, -steps), min(count, count - steps))
    return lax.ppermute(value, axis, [(source, source + steps) for source in range(leading, last)])


def mask_block(window_mask, width):
    upper, lower = (window_mask[0, tile, 0].astype(jnp.bfloat16) for tile in range(2))
    rows = [jnp.pad(row, (32 * slot, width - 32 * slot - 27)) for slot, row in enumerate((upper, lower, lower, upper))]
    return jnp.pad(jnp.stack(rows), ((0, MASK_ROWS - 4), (0, 0)))


def near_valid(row_valid):
    padded = jnp.pad(row_valid, ((TF, TF), (4, 4)))
    near = lax.dynamic_slice(padded, (lax.axis_index("tm") * TF, lax.axis_index("row") * 4), (3 * TF, 12))
    flat = jnp.pad(near.reshape(1, 72), ((0, 0), (0, 56)))
    return jnp.broadcast_to(flat, (16, 128)).astype(jnp.bfloat16)


def whole():
    return pl.BlockSpec(memory_space=pltpu.VMEM)


def shards(queries, key_states, value_states, grad_output, window_mask, row_valid):
    features = queries.shape[3]
    query, key, value, grad = (x.reshape(OWN, features) for x in (queries, key_states, value_states, grad_output))
    valid = near_valid(row_valid)
    picks = [jnp.asarray(x, jnp.bfloat16) for x in selectors()]
    parts = []
    for first, heads in GROUPS:
        lanes = slice(first * HD, (first + heads) * HD)
        width = heads * HD
        pair = jnp.concatenate([key[:, lanes], value[:, lanes]])
        low, high = shifted(pair, "tm", 1), shifted(pair, "tm", -1)
        message = jnp.concatenate(
            [low[:OWN], key[:, lanes], high[:OWN], low[OWN:], value[:, lanes], high[OWN:]]
            + [query[:, lanes], grad[:, lanes], mask_block(window_mask, width)]
        )
        above, below = shifted(message, "row", 1), shifted(message, "row", -1)
        output, grad_query, own_sum, low_sum, high_sum = pl.pallas_call(
            functools.partial(attend, heads),
            out_shape=(
                jax.ShapeDtypeStruct((OWN, width), jnp.bfloat16),
                jax.ShapeDtypeStruct((OWN, width), jnp.bfloat16),
                jax.ShapeDtypeStruct((2 * OWN, width), jnp.float32),
                jax.ShapeDtypeStruct((2 * OWN, width), jnp.bfloat16),
                jax.ShapeDtypeStruct((2 * OWN, width), jnp.bfloat16),
            ),
            in_specs=[whole()] * 7,
            out_specs=(whole(),) * 5,
            compiler_params=pltpu.CompilerParams(vmem_limit_bytes=40 * 1024 * 1024),
            cost_estimate=pl.CostEstimate(flops=heads * 400_000_000, bytes_accessed=8_000_000, transcendentals=0),
        )(message, above, below, valid, *picks)
        total = own_sum + shifted(low_sum, "tm", -1).astype(jnp.float32) + shifted(high_sum, "tm", 1).astype(jnp.float32)
        parts.append((output, grad_query, total[:OWN].astype(jnp.bfloat16), total[OWN:].astype(jnp.bfloat16)))
    return tuple(jnp.concatenate(pieces, axis=1).reshape(queries.shape) for pieces in zip(*parts))


def solution(mesh):
    placed = P("tm", "row", None, "head")
    return jax.shard_map(
        shards,
        mesh=mesh,
        in_specs=(placed, placed, placed, placed, P("tm", "row", None, None), P()),
        out_specs=(placed,) * 4,
        check_vma=False,
    )
```

time: 126 us -> 59.5 us (0.47)
  the two profiles are of different devices: /device:TPU:486 before, /device:TPU:476 now
where the time goes in v1:
time: 59.5 us; the launch traced here: 59.1 us
  waiting for transfers between devices  35.8 us (60%)
  starting transfers between devices  12 us (20%)
  Pallas kernels  6.46 us (11%)
  local copies, waits for them, and re-layouts  2.09 us (4%)
  other arithmetic  1.98 us (3%)
  between operations  0.87 us (1%)
    ppermute x6, waiting for transfers between devices, shifted(): lax.ppermute(value, axis, [(source, source + steps) for source in range(l...  35.8 us
    ppermute x6, starting transfers between devices, shifted(): lax.ppermute(value, axis, [(source, source + steps) for source in range(l...  12 us
    pallas_call x1, Pallas kernels, shards(): pl.pallas_call(functools.partial(attend, heads), out_shape=(jax.ShapeDtyp...  6.46 us
  transfers between devices with their start and end apart: 6, of which 5 were waited for; matrix products, arithmetic and copies ran while one was open for 3% of the time, Pallas kernels for 0%

profile of v1, /device:TPU:476, one launch (start us, length us, event | category | flops | bytes accessed | tf_op | source)
XLA Modules:
  0.0 59.1 jit_solution(747690640390667125)
XLA Ops:
  0.7 1.1 %pad_maximum_fusion = bf16[256,640]{1,0:T(8,128)(2,1)S(1)} fusion(bf16[128,640]{1,0:T(8,128)(2,1)} %bitcast.16, bf16[128,640]{1,0:T(8,128)(2,1)} %bitcast.14), kind=kLoop, calls=%fused_computation.1 | loop fusion | flops 655360 | bytes 655360 | tf_op jit(solution)/shard_map/concatenate | solution.py:197
  1.7 0.0 copy-start.5
  1.7 2.6 %collective-permute-start.1 = (bf16[256,640]{1,0:T(8,128)(2,1)S(1)}, bf16[256,640]{1,0:T(8,128)(2,1)S(1)}, u32[]{:S(2)}, u32[]{:S(2)}) collective-permute-start(bf16[256,640]{1,0:T(8,128)(2,1)S(1)} %pad_maximum_fusion), channel_id=1, source_target_pairs={{128,0},{256,128},{384,256},{129,1},{257,129},{385,257},{130,2},{2... | collective-permute-start | bytes 983048 | tf_op jit(solution)/shard_map/ppermute | solution.py:168
  4.4 1.3 %collective-permute-start = (bf16[256,640]{1,0:T(8,128)(2,1)S(1)}, bf16[256,640]{1,0:T(8,128)(2,1)S(1)}, u32[]{:S(2)}, u32[]{:S(2)}) collective-permute-start(bf16[256,640]{1,0:T(8,128)(2,1)S(1)} %pad_maximum_fusion), channel_id=1, source_target_pairs={{0,128},{128,256},{256,384},{1,129},{129,257},{257,385},{2,130},{1... | collective-permute-start | bytes 983048 | tf_op jit(solution)/shard_map/ppermute | solution.py:168
  5.7 0.7 %convert.13 = bf16[1,2,1,27]{3,2,1,0:T(2,128)(2,1)S(1)} convert(s32[1,2,1,27]{3,2,1,0:T(1,128)} %param.13) | non-fusion elementwise | flops 54 | bytes 324 | tf_op jit(solution)/shard_map/convert.6
  6.3 0.1 fusion.10
  6.5 0.0 copy-start
  6.5 0.0 copy-start.1
  6.5 0.0 copy-start.2
  6.5 8.9 %collective-permute-done = bf16[256,640]{1,0:T(8,128)(2,1)S(1)} collective-permute-done((bf16[256,640]{1,0:T(8,128)(2,1)S(1)}, bf16[256,640]{1,0:T(8,128)(2,1)S(1)}, u32[]{:S(2)}, u32[]{:S(2)}) %collective-permute-start) | collective-permute-done | bytes 327712 | tf_op jit(solution)/shard_map/ppermute | solution.py:168
  15.4 0.9 %constant_dynamic-update-slice_fusion.3 = bf16[1040,640]{1,0:T(8,128)(2,1)S(1)} fusion(bf16[1040,640]{1,0:T(8,128)(2,1)S(1)} %slice_dynamic-update-slice_fusion.3, bf16[128,640]{1,0:T(8,128)(2,1)} %bitcast.15), kind=kLoop, calls=%fused_computation.18 | loop fusion | bytes 327680
  16.6 1.9 %collective-permute-start.3 = (bf16[1040,640]{1,0:T(8,128)(2,1)S(1)}, bf16[1040,640]{1,0:T(8,128)(2,1)S(1)}, u32[]{:S(2)}, u32[]{:S(2)}) collective-permute-start(bf16[1040,640]{1,0:T(8,128)(2,1)S(1)} %fusion.7.here), channel_id=1, source_target_pairs={{8,0},{16,8},{24,16},{32,24},{40,32},{48,40},{56,48},{64,56},{72,6... | collective-permute-start | bytes 3993608 | tf_op jit(solution)/shard_map/ppermute | solution.py:168
  18.6 2.4 %collective-permute-start.2 = (bf16[1040,640]{1,0:T(8,128)(2,1)S(1)}, bf16[1040,640]{1,0:T(8,128)(2,1)}, u32[]{:S(2)}, u32[]{:S(2)}) collective-permute-start(bf16[1040,640]{1,0:T(8,128)(2,1)S(1)} %fusion.7.here), channel_id=1, source_target_pairs={{0,8},{8,16},{16,24},{24,32},{32,40},{40,48},{48,56},{56,64},{64,7... | collective-permute-start | bytes 3993608 | tf_op jit(solution)/shard_map/ppermute | solution.py:168
  21.0 0.1 fusion.8
  21.1 0.1 reshape.43
  21.2 12.7 %collective-permute-done.3.below = bf16[1040,640]{1,0:T(8,128)(2,1)S(1)} collective-permute-done((bf16[1040,640]{1,0:T(8,128)(2,1)S(1)}, bf16[1040,640]{1,0:T(8,128)(2,1)S(1)}, u32[]{:S(2)}, u32[]{:S(2)}) %collective-permute-start.3) | collective-permute-done | bytes 1331232 | tf_op jit(solution)/shard_map/ppermute | solution.py:168
  33.9 3.9 %collective-permute-done.2.above = bf16[1040,640]{1,0:T(8,128)(2,1)} collective-permute-done((bf16[1040,640]{1,0:T(8,128)(2,1)S(1)}, bf16[1040,640]{1,0:T(8,128)(2,1)}, u32[]{:S(2)}, u32[]{:S(2)}) %collective-permute-start.2) | collective-permute-done | bytes 1331232 | tf_op jit(solution)/shard_map/ppermute | solution.py:168
  37.8 6.5 %shard_map.120 = (bf16[128,640]{1,0:T(8,128)(2,1)}, bf16[128,640]{1,0:T(8,128)(2,1)}, f32[256,640]{1,0:T(8,128)S(1)}, bf16[256,640]{1,0:T(8,128)(2,1)S(1)}, bf16[256,640]{1,0:T(8,128)(2,1)S(1)}) custom-call(bf16[1040,640]{1,0:T(8,128)(2,1)S(1)} %fusion.7.here, bf16[1040,640]{1,0:T(8,128)(2,1)} %collective-permute-done.2.above, ...), custom_call_target="tpu_custom_call" | custom-call | flops 2000000000 | bytes 8000000 | tf_op jit(solution)/shard_map/pallas_call | solution.py:204
  44.3 2.4 %collective-permute-start.4 = (bf16[256,640]{1,0:T(8,128)(2,1)S(1)}, bf16[256,640]{1,0:T(8,128)(2,1)S(1)}, u32[]{:S(2)}, u32[]{:S(2)}) collective-permute-start(bf16[256,640]{1,0:T(8,128)(2,1)S(1)} %get-tuple-element.12), channel_id=1, source_target_pairs={{128,0},{256,128},{384,256},{129,1},{257,129},{385,257},{130,2},{2... | collective-permute-start | bytes 983048 | tf_op jit(solution)/shard_map/ppermute | solution.py:168
  46.7 1.3 %collective-permute-start.5 = (bf16[256,640]{1,0:T(8,128)(2,1)S(1)}, bf16[256,640]{1,0:T(8,128)(2,1)S(1)}, u32[]{:S(2)}, u32[]{:S(2)}) collective-permute-start(bf16[256,640]{1,0:T(8,128)(2,1)S(1)} %get-tuple-element.13), channel_id=1, source_target_pairs={{0,128},{128,256},{256,384},{1,129},{129,257},{257,385},{2,130},{1... | collective-permute-start | bytes 983048 | tf_op jit(solution)/shard_map/ppermute | solution.py:168
  48.0 6.1 %collective-permute-done.4 = bf16[256,640]{1,0:T(8,128)(2,1)S(1)} collective-permute-done((bf16[256,640]{1,0:T(8,128)(2,1)S(1)}, bf16[256,640]{1,0:T(8,128)(2,1)S(1)}, u32[]{:S(2)}, u32[]{:S(2)}) %collective-permute-start.4) | collective-permute-done | bytes 327712 | tf_op jit(solution)/shard_map/ppermute | solution.py:168
  54.2 4.1 %collective-permute-done.5 = bf16[256,640]{1,0:T(8,128)(2,1)S(1)} collective-permute-done((bf16[256,640]{1,0:T(8,128)(2,1)S(1)}, bf16[256,640]{1,0:T(8,128)(2,1)S(1)}, u32[]{:S(2)}, u32[]{:S(2)}) %collective-permute-start.5) | collective-permute-done | bytes 327712 | tf_op jit(solution)/shard_map/ppermute | solution.py:168
  58.3 0.1 add_convert_fusion
  58.4 0.8 %fusion.9 = (bf16[128,640]{1,0:T(8,128)(2,1)}, bf16[128,640]{1,0:T(8,128)(2,1)}) fusion(bf16[256,640]{1,0:T(8,128)(2,1)S(1)} %add_convert_fusion), kind=kLoop, calls=%fused_computation.24 | loop fusion | bytes 655360 | tf_op jit(solution)/shard_map/slice | solution.py:219
  (26 shorter events, 0.2 us)
Async XLA Ops:
  0.6 15.8 %copy-start.3 = (bf16[2,4,16,640]{3,2,1,0:T(8,128)(2,1)S(1)}, bf16[2,4,16,640]{3,2,1,0:T(8,128)(2,1)}, u32[]{:S(2)}) copy-start(bf16[2,4,16,640]{3,2,1,0:T(8,128)(2,1)} %param.11) | copy-start | bytes 491524
  0.6 15.9 %copy-start.4 = (bf16[2,4,16,640]{3,2,1,0:T(8,128)(2,1)S(1)}, bf16[2,4,16,640]{3,2,1,0:T(8,128)(2,1)}, u32[]{:S(2)}) copy-start(bf16[2,4,16,640]{3,2,1,0:T(8,128)(2,1)} %param.9) | copy-start | bytes 491524
  1.7 14.8 %copy-start.5 = (bf16[2,4,16,640]{3,2,1,0:T(8,128)(2,1)S(1)}, bf16[2,4,16,640]{3,2,1,0:T(8,128)(2,1)}, u32[]{:S(2)}) copy-start(bf16[2,4,16,640]{3,2,1,0:T(8,128)(2,1)} %param.12) | copy-start | bytes 491524
  1.7 14.6 %collective-permute-start.1 = (bf16[256,640]{1,0:T(8,128)(2,1)S(1)}, bf16[256,640]{1,0:T(8,128)(2,1)S(1)}, u32[]{:S(2)}, u32[]{:S(2)}) collective-permute-start(bf16[256,640]{1,0:T(8,128)(2,1)S(1)} %pad_maximum_fusion), channel_id=1, source_target_pairs={{128,0},{256,128},{384,256},{129,1},{257,129},{385,257},{130,2},{2... | collective-permute-start | bytes 983048 | tf_op jit(solution)/shard_map/ppermute | solution.py:168
  4.4 11.1 %collective-permute-start = (bf16[256,640]{1,0:T(8,128)(2,1)S(1)}, bf16[256,640]{1,0:T(8,128)(2,1)S(1)}, u32[]{:S(2)}, u32[]{:S(2)}) collective-permute-start(bf16[256,640]{1,0:T(8,128)(2,1)S(1)} %pad_maximum_fusion), channel_id=1, source_target_pairs={{0,128},{128,256},{256,384},{1,129},{129,257},{257,385},{2,130},{1... | collective-permute-start | bytes 983048 | tf_op jit(solution)/shard_map/ppermute | solution.py:168
  6.5 14.5 %copy-start.6 = (s32[8,64]{1,0:T(8,128)S(1)}, s32[8,64]{1,0:T(8,128)}, u32[]{:S(2)}) copy-start(s32[8,64]{1,0:T(8,128)} %param.14) | copy-start | bytes 6148
  6.5 31.3 %copy-start = (bf16[128,1536]{1,0:T(8,128)(2,1)S(1)}, bf16[128,1536]{1,0:T(8,128)(2,1)}, u32[]{:S(2)}) copy-start(bf16[128,1536]{1,0:T(8,128)(2,1)} %constant.31.clone.valid_pick) | copy-start | bytes 1179652
  6.5 31.3 %copy-start.1 = (bf16[128,768]{1,0:T(8,128)(2,1)S(1)}, bf16[128,768]{1,0:T(8,128)(2,1)}, u32[]{:S(2)}) copy-start(bf16[128,768]{1,0:T(8,128)(2,1)} %constant.30.clone.mask_pick) | copy-start | bytes 589828
  6.5 31.3 %copy-start.2 = (bf16[256,128]{1,0:T(8,128)(2,1)S(1)}, bf16[256,128]{1,0:T(8,128)(2,1)}, u32[]{:S(2)}) copy-start(bf16[256,128]{1,0:T(8,128)(2,1)} %constant.32.clone.query_pick) | copy-start | bytes 196612
  16.6 17.3 %collective-permute-start.3 = (bf16[1040,640]{1,0:T(8,128)(2,1)S(1)}, bf16[1040,640]{1,0:T(8,128)(2,1)S(1)}, u32[]{:S(2)}, u32[]{:S(2)}) collective-permute-start(bf16[1040,640]{1,0:T(8,128)(2,1)S(1)} %fusion.7.here), channel_id=1, source_target_pairs={{8,0},{16,8},{24,16},{32,24},{40,32},{48,40},{56,48},{64,56},{72,6... | collective-permute-start | bytes 3993608 | tf_op jit(solution)/shard_map/ppermute | solution.py:168
  18.6 19.3 %collective-permute-start.2 = (bf16[1040,640]{1,0:T(8,128)(2,1)S(1)}, bf16[1040,640]{1,0:T(8,128)(2,1)}, u32[]{:S(2)}, u32[]{:S(2)}) collective-permute-start(bf16[1040,640]{1,0:T(8,128)(2,1)S(1)} %fusion.7.here), channel_id=1, source_target_pairs={{0,8},{8,16},{16,24},{24,32},{32,40},{40,48},{48,56},{56,64},{64,7... | collective-permute-start | bytes 3993608 | tf_op jit(solution)/shard_map/ppermute | solution.py:168
  44.3 9.9 %collective-permute-start.4 = (bf16[256,640]{1,0:T(8,128)(2,1)S(1)}, bf16[256,640]{1,0:T(8,128)(2,1)S(1)}, u32[]{:S(2)}, u32[]{:S(2)}) collective-permute-start(bf16[256,640]{1,0:T(8,128)(2,1)S(1)} %get-tuple-element.12), channel_id=1, source_target_pairs={{128,0},{256,128},{384,256},{129,1},{257,129},{385,257},{130,2},{2... | collective-permute-start | bytes 983048 | tf_op jit(solution)/shard_map/ppermute | solution.py:168
  46.7 11.5 %collective-permute-start.5 = (bf16[256,640]{1,0:T(8,128)(2,1)S(1)}, bf16[256,640]{1,0:T(8,128)(2,1)S(1)}, u32[]{:S(2)}, u32[]{:S(2)}) collective-permute-start(bf16[256,640]{1,0:T(8,128)(2,1)S(1)} %get-tuple-element.13), channel_id=1, source_target_pairs={{0,128},{128,256},{256,384},{1,129},{129,257},{257,385},{2,130},{1... | collective-permute-start | bytes 983048 | tf_op jit(solution)/shard_map/ppermute | solution.py:168

commit v2 on v1

v2 whole, which is shorter than its diff:
```python
import functools
import math

import jax
import jax.numpy as jnp
from jax import lax
from jax.experimental import pallas as pl
from jax.experimental.pallas import tpu as pltpu
from jax.sharding import PartitionSpec as P

HD = 128
TF = 2
BAND = 64
HALF = BAND // 2
OWN = TF * BAND
TILE = TF * HALF
NEAR = 3 * OWN
MASK_ROWS = 16
GROUPS = ((0, 5),)
LATE = 2

SCALE = HD ** (-0.5)
SCALE_LOG2 = SCALE * math.log2(math.e)
FAR = 1e30


def contract(left, right, dims):
    return lax.dot_general(left, right, ((dims[:1], dims[1:]), ((), ())), preferred_element_type=jnp.float32)


SLOT_TILE = (2, 3, 1, 4)


def other_tile(slot, half):
    return ((1, 4), (1, 4), (0, 1), (4, 5))[slot][half]


def lane_facts(lanes):
    lane = lax.broadcasted_iota(jnp.int32, (1, lanes), 1)
    return lane // BAND, lane % BAND // HALF, lane % HALF // 16


def mask_places():
    frame, half, _ = lane_facts(NEAR)
    blocks = []
    for slot in range(4):
        at = []
        for tile in (2 + half, jnp.where(half == 0, other_tile(slot, 0), other_tile(slot, 1))):
            step = tile - SLOT_TILE[slot]
            at.append(jnp.where(jnp.abs(step) <= 1, 9 * (frame // TF) + 3 * (step + 1) + 1, -1))
        at = jnp.concatenate(at, axis=1)
        entry = lax.broadcasted_iota(jnp.int32, (32, 2 * NEAR), 0)
        blocks.append((entry == at).astype(jnp.float32))
    return jnp.concatenate(blocks).astype(jnp.bfloat16)


def live_keys(row_valid, first_frame, first_row):
    frame, half, row = lane_facts(NEAR)
    rows = [4 + 2 * half + row]
    rows += [2 * jnp.where(half == 0, other_tile(slot, 0), other_tile(slot, 1)) + row for slot in (0, 2, 3)]
    rows = jnp.concatenate(rows, axis=1) + first_row
    frames = jnp.concatenate([frame] * 4, axis=1) + first_frame
    count, here = row_valid.shape
    pick = (lax.broadcasted_iota(jnp.int32, (here, 4 * NEAR), 0) == rows).astype(jnp.float32)
    found = contract(row_valid, pick, (1, 0))
    return jnp.sum(jnp.where(lax.broadcasted_iota(jnp.int32, (count, 4 * NEAR), 0) == frames, found, 0.0), axis=0, keepdims=True)


def live_queries(row_valid, first_frame, first_row):
    count, here = row_valid.shape
    token = lax.broadcasted_iota(jnp.int32, (4 * TILE, 1), 0)
    slot = token // TILE
    tile = jnp.where(slot < 2, slot + 2, jnp.where(slot == 2, 1, 4))
    frames = first_frame + TF + token % TILE // HALF
    rows = first_row + 2 * tile + token % HALF // 16
    pick = (lax.broadcasted_iota(jnp.int32, (4 * TILE, here), 1) == rows).astype(jnp.float32)
    found = contract(pick, row_valid, (1, 1))
    return jnp.sum(jnp.where(lax.broadcasted_iota(jnp.int32, (4 * TILE, count), 1) == frames, found, 0.0), axis=1, keepdims=True)


def row_tile(block, half):
    return jnp.concatenate([block[f * BAND + half * HALF : f * BAND + (half + 1) * HALF] for f in range(TF)])


def beside(above, below):
    parts = []
    for start in range(0, NEAR, BAND):
        parts += [above[start + HALF : start + BAND], below[start : start + HALF]]
    return jnp.concatenate(parts)


def store_tiles(ref, value, lanes):
    for half in range(2):
        for frame in range(TF):
            start = frame * BAND + half * HALF
            source = half * TILE + frame * HALF
            ref[start : start + HALF, lanes] = value[source : source + HALF]


def attend(heads, first, *refs):
    (query_ref, key_ref, value_ref, grad_ref, low, high, above, below), refs = refs[:8], refs[8:]
    far_above, far_below, refs = refs[:LATE], refs[LATE : 2 * LATE], refs[2 * LATE :]
    (window_mask, row_valid), refs = refs[:2], refs[2:]
    output, grad_query, own_sum, low_sum, high_sum, held = refs

    mask_at = 2 * OWN + 2 * TILE
    here, up, down = (
        block.astype(jnp.float32)
        for block in (
            padded_masks(window_mask, held),
            above[mask_at : mask_at + MASK_ROWS, :128],
            below[mask_at : mask_at + MASK_ROWS, :128],
        )
    )
    sources = (here[0:1], here[1:2], up[1:2], down[0:1])
    slot = lax.broadcasted_iota(jnp.int32, (MASK_ROWS, 128), 0)
    masks = jnp.zeros((MASK_ROWS, 128), jnp.float32)
    for index, source in enumerate(sources):
        row = jnp.broadcast_to(source, (MASK_ROWS, 128))
        masks = jnp.where(slot == index, pltpu.roll(row, 32 * index, 1), masks)
    kept = contract(masks.astype(jnp.bfloat16), mask_places(), (1, 0))
    first_frame = (lax.axis_index("tm") - 1) * TF
    first_row = (lax.axis_index("row") - 1) * 4
    row_valid = row_valid[...].astype(jnp.float32)
    live = live_keys(row_valid, first_frame, first_row)
    query_live = live_queries(row_valid, first_frame, first_row)
    bias_own, bias_other = [], []
    for index in range(4):
        part = max(index - 1, 0) + 1
        keep_own = kept[index : index + 1, :NEAR] * live[:1, :NEAR]
        keep_other = kept[index : index + 1, NEAR:] * live[:1, part * NEAR : (part + 1) * NEAR]
        bias_own.append(jnp.broadcast_to((keep_own - 1.0) * FAR, (TILE, NEAR)))
        bias_other.append(jnp.broadcast_to((keep_other - 1.0) * FAR, (TILE, NEAR)))
    bias_own = jnp.concatenate(bias_own)
    bias_other = jnp.concatenate(bias_other)

    def far(refs, side, part, lanes):
        ref = refs[side % LATE]
        start = (side * 2 * OWN if LATE == 1 else 0) + part * OWN
        return ref[start : start + OWN, lanes]

    for head in range(heads):
        lanes = slice(head * HD, (head + 1) * HD)
        arg_lanes = slice((first + head) * HD, (first + head + 1) * HD)
        query_own, grad_own = query_ref[:, arg_lanes], grad_ref[:, arg_lanes]
        at = 2 * OWN
        query = jnp.concatenate(
            [row_tile(query_own, 0), row_tile(query_own, 1), above[at : at + TILE, lanes], below[at : at + TILE, lanes]]
        )
        at += TILE
        grad = jnp.concatenate(
            [row_tile(grad_own, 0), row_tile(grad_own, 1), above[at : at + TILE, lanes], below[at : at + TILE, lanes]]
        )

        def region(part, ref):
            rows = slice(part * OWN, (part + 1) * OWN)
            here = jnp.concatenate([low[rows, lanes], ref[:, arg_lanes], high[rows, lanes]])
            up = jnp.concatenate([far(far_above, 0, part, lanes), above[rows, lanes], far(far_above, 1, part, lanes)])
            down = jnp.concatenate([far(far_below, 0, part, lanes), below[rows, lanes], far(far_below, 1, part, lanes)])
            return here, up, down, beside(up, down)

        key_own, key_up, key_down, key_side = region(0, key_ref)
        value_own, value_up, value_down, value_side = region(1, value_ref)

        score_own = contract(query, key_own, (1, 1)) * SCALE_LOG2 + bias_own
        score_other = (
            jnp.concatenate(
                [
                    contract(query[:OWN], key_side, (1, 1)),
                    contract(query[OWN : OWN + TILE], key_up, (1, 1)),
                    contract(query[OWN + TILE :], key_down, (1, 1)),
                ]
            )
            * SCALE_LOG2
            + bias_other
        )
        row_max = jnp.max(jnp.maximum(score_own, score_other), axis=1, keepdims=True)
        own = jnp.exp2(score_own - row_max)
        other = jnp.exp2(score_other - row_max)
        share = query_live / jnp.sum(own + other, axis=1, keepdims=True)
        own_bf, other_bf = own.astype(jnp.bfloat16), other.astype(jnp.bfloat16)
        attended = contract(own_bf, value_own, (1, 0)) + jnp.concatenate(
            [
                contract(other_bf[:OWN], value_side, (1, 0)),
                contract(other_bf[OWN : OWN + TILE], value_up, (1, 0)),
                contract(other_bf[OWN + TILE :], value_down, (1, 0)),
            ]
        )
        result = (attended * share).astype(jnp.bfloat16)
        row_dot = jnp.sum(result.astype(jnp.float32) * grad.astype(jnp.float32), axis=1, keepdims=True)
        weight_own = own * share
        weight_side = other[:OWN] * share[:OWN]
        grad_score_own = (weight_own * (contract(grad, value_own, (1, 1)) - row_dot)).astype(jnp.bfloat16)
        grad_score_side = (weight_side * (contract(grad[:OWN], value_side, (1, 1)) - row_dot[:OWN])).astype(jnp.bfloat16)
        query_sum = contract(grad_score_own[:OWN], key_own, (1, 0)) + contract(grad_score_side, key_side, (1, 0))
        key_sum = contract(grad_score_own, query, (0, 0)) * SCALE
        value_sum = contract(weight_own.astype(jnp.bfloat16), grad, (0, 0))

        store_tiles(output, result, lanes)
        store_tiles(grad_query, (query_sum * SCALE).astype(jnp.bfloat16), lanes)
        for part, total in enumerate((key_sum, value_sum)):
            rows = slice(part * OWN, (part + 1) * OWN)
            low_sum[rows, lanes] = total[:OWN].astype(jnp.bfloat16)
            own_sum[rows, lanes] = total[OWN : 2 * OWN]
            high_sum[rows, lanes] = total[2 * OWN :].astype(jnp.bfloat16)


def shifted(value, axis, steps):
    count = lax.axis_size(axis)
    leading, last = (max(0, -steps), min(count, count - steps))
    return lax.ppermute(value, axis, [(source, source + steps) for source in range(leading, last)])


def ring(value, axis, steps):
    count = lax.axis_size(axis)
    return lax.ppermute(value, axis, [(source, (source + steps) % count) for source in range(count)])


def padded_masks(window_mask, held):
    held[...] = jnp.zeros_like(held)
    for tile in range(2):
        held[tile : tile + 1, :27] = window_mask[0, tile].astype(jnp.float32)
    return held[...]


def pack(first, heads, query, key, value, grad, window_mask, pair, near_up, near_down, stage, held, block, sems):
    lanes = slice(first * HD, (first + heads) * HD)
    loads, copies = [], []
    for part, ref in enumerate((key, value, query, grad)):
        loads.append(pltpu.make_async_copy(ref.at[:, lanes], stage.at[part], sems.at[part]))
        loads[-1].start()

    def copy(source, target):
        copies.append(pltpu.make_async_copy(source, target, sems.at[4 + len(copies)]))
        copies[-1].start()

    block[...] = padded_masks(window_mask, held).astype(jnp.bfloat16)
    rows = slice(2 * OWN + 2 * TILE, 2 * OWN + 2 * TILE + MASK_ROWS)
    for target in (near_up, near_down):
        copy(block, target.at[rows, :128])
    for part in range(2):
        loads[part].wait()
        rows = slice(part * OWN, (part + 1) * OWN)
        for target in (pair, near_up, near_down):
            copy(stage.at[part], target.at[rows])
    for part in range(2):
        loads[2 + part].wait()
        for half, target in enumerate((near_down, near_up)):
            for frame in range(TF):
                at = 2 * OWN + part * TILE + frame * HALF
                start = frame * BAND + half * HALF
                copy(stage.at[2 + part, start : start + HALF], target.at[at : at + HALF])
    for started in copies:
        started.wait()


def whole():
    return pl.BlockSpec(memory_space=pltpu.VMEM)


def shards(queries, key_states, value_states, grad_output, window_mask, row_valid):
    features = queries.shape[3]
    query, key, value, grad = (x.reshape(OWN, features) for x in (queries, key_states, value_states, grad_output))
    parts = []
    for first, heads in GROUPS:
        width = heads * HD
        pair, near_up, near_down = pl.pallas_call(
            functools.partial(pack, first, heads),
            out_shape=[
                jax.ShapeDtypeStruct((rows, width), jnp.bfloat16)
                for rows in (2 * OWN, *[2 * OWN + 2 * TILE + MASK_ROWS] * 2)
            ],
            in_specs=[pl.BlockSpec(memory_space=pl.ANY)] * 4 + [whole()],
            out_specs=[pl.BlockSpec(memory_space=pl.ANY)] * 3,
            scratch_shapes=[
                pltpu.VMEM((4, OWN, width), jnp.bfloat16),
                pltpu.VMEM((MASK_ROWS, 128), jnp.float32),
                pltpu.VMEM((MASK_ROWS, 128), jnp.bfloat16),
                pltpu.SemaphoreType.DMA((20,)),
            ],
            cost_estimate=pl.CostEstimate(flops=0, bytes_accessed=2_000_000, transcendentals=0),
        )(query, key, value, grad, window_mask)
        low, high = shifted(pair, "tm", 1), shifted(pair, "tm", -1)
        above, below = ring(near_up, "row", 1), ring(near_down, "row", -1)
        far = [jnp.concatenate([low, high])] if LATE == 1 else [low, high]
        far_above = [ring(x, "row", 1) for x in far]
        far_below = [ring(x, "row", -1) for x in far]
        output, grad_query, own_sum, low_sum, high_sum = pl.pallas_call(
            functools.partial(attend, heads, first),
            out_shape=(
                jax.ShapeDtypeStruct((OWN, width), jnp.bfloat16),
                jax.ShapeDtypeStruct((OWN, width), jnp.bfloat16),
                jax.ShapeDtypeStruct((2 * OWN, width), jnp.float32),
                jax.ShapeDtypeStruct((2 * OWN, width), jnp.bfloat16),
                jax.ShapeDtypeStruct((2 * OWN, width), jnp.bfloat16),
            ),
            in_specs=[whole()] * (10 + 2 * LATE),
            out_specs=(whole(),) * 5,
            scratch_shapes=[pltpu.VMEM((MASK_ROWS, 128), jnp.float32)],
            compiler_params=pltpu.CompilerParams(vmem_limit_bytes=40 * 1024 * 1024),
            cost_estimate=pl.CostEstimate(flops=heads * 400_000_000, bytes_accessed=8_000_000, transcendentals=0),
        )(query, key, value, grad, low, high, above, below, *far_above, *far_below, window_mask, row_valid)
        total = own_sum + shifted(low_sum, "tm", -1).astype(jnp.float32) + shifted(high_sum, "tm", 1).astype(jnp.float32)
        parts.append((output, grad_query, total[:OWN].astype(jnp.bfloat16), total[OWN:].astype(jnp.bfloat16)))
    return tuple(jnp.concatenate(pieces, axis=1).reshape(queries.shape) for pieces in zip(*parts))


def solution(mesh):
    placed = P("tm", "row", None, "head")
    return jax.shard_map(
        shards,
        mesh=mesh,
        in_specs=(placed, placed, placed, placed, P("tm", "row", None, None), P()),
        out_specs=(placed,) * 4,
        check_vma=False,
    )
```

time: 59.5 us -> 48.8 us (0.82)
  the two profiles are of different devices: /device:TPU:476 before, /device:TPU:57 now
where the time goes in v2:
time: 48.8 us; the launch traced here: 48.6 us
  starting transfers between devices  22.1 us (45%)
  waiting for transfers between devices  16.6 us (34%)
  Pallas kernels  8.24 us (17%)
  local copies, waits for them, and re-layouts  0.78 us (2%)
  between operations  0.77 us (2%)
    ppermute x6, starting transfers between devices, ring(): lax.ppermute(value, axis, [(source, (source + steps) % count) for source...  11.4 us
    ppermute x4, starting transfers between devices, shifted(): lax.ppermute(value, axis, [(source, source + steps) for source in range(l...  10.7 us
    ppermute x4, waiting for transfers between devices, shifted(): lax.ppermute(value, axis, [(source, source + steps) for source in range(l...  8.32 us
    ppermute x6, waiting for transfers between devices, ring(): lax.ppermute(value, axis, [(source, (source + steps) % count) for source...  8.3 us
    pallas_call x1, Pallas kernels, shards(): pl.pallas_call(functools.partial(attend, heads, first), out_shape=(jax.Sh...  5.34 us
    pallas_call x1, Pallas kernels, shards(): pl.pallas_call(functools.partial(pack, first, heads), out_shape=[jax.Shap...  2.91 us
  transfers between devices with their start and end apart: 10, of which 6 were waited for; matrix products, arithmetic and copies ran while one was open for 0% of the time, Pallas kernels for 0%

profile of v2, /device:TPU:57, one launch (start us, length us, event | category | flops | bytes accessed | tf_op | source)
XLA Modules:
  0.0 48.6 jit_solution(3010665340558692654)
XLA Ops:
  0.7 2.9 %shard_map.93 = (bf16[256,640]{1,0:T(8,128)(2,1)}, bf16[400,640]{1,0:T(8,128)(2,1)}, bf16[400,640]{1,0:T(8,128)(2,1)}) custom-call(bf16[128,640]{1,0:T(8,128)(2,1)} %bitcast.8, bf16[128,640]{1,0:T(8,128)(2,1)} %bitcast.10, bf16[128,640]{1,0:T(8,128)(2,1)} %bitcast.12, bf16[128,640]{1,0:T(8,128)(2,1)} %bitcast.14, s32[1,2,1,27]{3,2,1,0:T(1,128)} %refs_12_.1), custom_call_target="tpu_custom_call" | custom-call | bytes 2000000 | tf_op jit(solution)/shard_map/pallas_call | solution.py:267
  3.6 0.0 copy-start.5
  3.6 5.4 %collective-permute-start.2 = (bf16[400,640]{1,0:T(8,128)(2,1)}, bf16[400,640]{1,0:T(8,128)(2,1)S(1)}, u32[]{:S(2)}, u32[]{:S(2)}) collective-permute-start(bf16[400,640]{1,0:T(8,128)(2,1)} %get-tuple-element.13), channel_id=1, source_target_pairs={{0,8},{8,16},{16,24},{24,32},{32,40},{40,48},{48,56},{56,64},{64,7... | collective-permute-start | bytes 1536008 | tf_op jit(solution)/shard_map/ppermute | solution.py:216
  9.0 1.4 %collective-permute-start.1 = (bf16[256,640]{1,0:T(8,128)(2,1)}, bf16[256,640]{1,0:T(8,128)(2,1)S(1)}, u32[]{:S(2)}, u32[]{:S(2)}) collective-permute-start(bf16[256,640]{1,0:T(8,128)(2,1)} %get-tuple-element.12), channel_id=1, source_target_pairs={{128,0},{256,128},{384,256},{129,1},{257,129},{385,257},{130,2},{2... | collective-permute-start | bytes 983048 | tf_op jit(solution)/shard_map/ppermute | solution.py:211
  10.5 4.0 %collective-permute-start = (bf16[256,640]{1,0:T(8,128)(2,1)}, bf16[256,640]{1,0:T(8,128)(2,1)S(1)}, u32[]{:S(2)}, u32[]{:S(2)}) collective-permute-start(bf16[256,640]{1,0:T(8,128)(2,1)} %get-tuple-element.12), channel_id=1, source_target_pairs={{0,128},{128,256},{256,384},{1,129},{129,257},{257,385},{2,130},{1... | collective-permute-start | bytes 983048 | tf_op jit(solution)/shard_map/ppermute | solution.py:211
  14.5 0.0 collective-permute-start.3
  14.5 2.7 %collective-permute-done.1.refs_5_ = bf16[256,640]{1,0:T(8,128)(2,1)S(1)} collective-permute-done((bf16[256,640]{1,0:T(8,128)(2,1)}, bf16[256,640]{1,0:T(8,128)(2,1)S(1)}, u32[]{:S(2)}, u32[]{:S(2)}) %collective-permute-start.1) | collective-permute-done | bytes 327712 | tf_op jit(solution)/shard_map/ppermute | solution.py:211
  17.2 0.0 collective-permute-start.7
  17.2 3.0 %collective-permute-start.5 = (bf16[256,640]{1,0:T(8,128)(2,1)S(1)}, bf16[256,640]{1,0:T(8,128)(2,1)S(1)}, u32[]{:S(2)}, u32[]{:S(2)}) collective-permute-start(bf16[256,640]{1,0:T(8,128)(2,1)S(1)} %collective-permute-done.1.refs_5_), channel_id=1, source_target_pairs={{0,8},{8,16},{16,24},{24,32},{32,40},{40,48},{48,56},{56,64},{64,7... | collective-permute-start | bytes 983048 | tf_op jit(solution)/shard_map/ppermute | solution.py:216
  20.1 0.0 collective-permute-done.refs_4_
  20.1 0.0 collective-permute-start.6
  20.1 0.0 collective-permute-done.2.refs_6_
  20.2 3.0 %collective-permute-start.4 = (bf16[256,640]{1,0:T(8,128)(2,1)S(1)}, bf16[256,640]{1,0:T(8,128)(2,1)S(1)}, u32[]{:S(2)}, u32[]{:S(2)}) collective-permute-start(bf16[256,640]{1,0:T(8,128)(2,1)S(1)} %collective-permute-done.refs_4_), channel_id=1, source_target_pairs={{0,8},{8,16},{16,24},{24,32},{32,40},{40,48},{48,56},{56,64},{64,7... | collective-permute-start | bytes 983048 | tf_op jit(solution)/shard_map/ppermute | solution.py:216
  23.1 1.3 %collective-permute-done.3.refs_7_ = bf16[400,640]{1,0:T(8,128)(2,1)S(1)} collective-permute-done((bf16[400,640]{1,0:T(8,128)(2,1)}, bf16[400,640]{1,0:T(8,128)(2,1)S(1)}, u32[]{:S(2)}, u32[]{:S(2)}) %collective-permute-start.3) | collective-permute-done | bytes 512032 | tf_op jit(solution)/shard_map/ppermute | solution.py:216
  24.4 3.5 %collective-permute-done.7.refs_11_ = bf16[256,640]{1,0:T(8,128)(2,1)S(1)} collective-permute-done((bf16[256,640]{1,0:T(8,128)(2,1)S(1)}, bf16[256,640]{1,0:T(8,128)(2,1)S(1)}, u32[]{:S(2)}, u32[]{:S(2)}) %collective-permute-start.7) | collective-permute-done | bytes 327712 | tf_op jit(solution)/shard_map/ppermute | solution.py:216
  27.9 0.0 collective-permute-done.5.refs_9_
  27.9 3.5 %collective-permute-done.6.refs_10_ = bf16[256,640]{1,0:T(8,128)(2,1)S(1)} collective-permute-done((bf16[256,640]{1,0:T(8,128)(2,1)S(1)}, bf16[256,640]{1,0:T(8,128)(2,1)S(1)}, u32[]{:S(2)}, u32[]{:S(2)}) %collective-permute-start.6) | collective-permute-done | bytes 327712 | tf_op jit(solution)/shard_map/ppermute | solution.py:216
  31.4 5.3 %shard_map.94 = (bf16[128,640]{1,0:T(8,128)(2,1)}, bf16[128,640]{1,0:T(8,128)(2,1)}, f32[256,640]{1,0:T(8,128)S(1)}, bf16[256,640]{1,0:T(8,128)(2,1)S(1)}, bf16[256,640]{1,0:T(8,128)(2,1)S(1)}) custom-call(bf16[128,640]{1,0:T(8,128)(2,1)S(1)} %bitcast.9, bf16[128,640]{1,0:T(8,128)(2,1)S(1)} %bitcast.11, bf16[128,640]{1,0:T(8,128)(2,1)S(1)} %bitcast.13, ...), custom_call_target="tpu_custom_call" | custom-call | flops 2000000000 | bytes 8000000 | tf_op jit(solution)/shard_map/pallas_call | solution.py:288
  36.8 1.3 %collective-permute-start.8 = (bf16[256,640]{1,0:T(8,128)(2,1)S(1)}, bf16[256,640]{1,0:T(8,128)(2,1)S(1)}, u32[]{:S(2)}, u32[]{:S(2)}) collective-permute-start(bf16[256,640]{1,0:T(8,128)(2,1)S(1)} %get-tuple-element.18), channel_id=1, source_target_pairs={{128,0},{256,128},{384,256},{129,1},{257,129},{385,257},{130,2},{2... | collective-permute-start | bytes 983048 | tf_op jit(solution)/shard_map/ppermute | solution.py:211
  38.1 4.0 %collective-permute-start.9 = (bf16[256,640]{1,0:T(8,128)(2,1)S(1)}, bf16[256,640]{1,0:T(8,128)(2,1)S(1)}, u32[]{:S(2)}, u32[]{:S(2)}) collective-permute-start(bf16[256,640]{1,0:T(8,128)(2,1)S(1)} %get-tuple-element.19), channel_id=1, source_target_pairs={{0,128},{128,256},{256,384},{1,129},{129,257},{257,385},{2,130},{1... | collective-permute-start | bytes 983048 | tf_op jit(solution)/shard_map/ppermute | solution.py:211
  42.1 3.9 %collective-permute-done.8 = bf16[256,640]{1,0:T(8,128)(2,1)S(1)} collective-permute-done((bf16[256,640]{1,0:T(8,128)(2,1)S(1)}, bf16[256,640]{1,0:T(8,128)(2,1)S(1)}, u32[]{:S(2)}, u32[]{:S(2)}) %collective-permute-start.8) | collective-permute-done | bytes 327712 | tf_op jit(solution)/shard_map/ppermute | solution.py:211
  46.0 1.8 %collective-permute-done.9 = bf16[256,640]{1,0:T(8,128)(2,1)S(1)} collective-permute-done((bf16[256,640]{1,0:T(8,128)(2,1)S(1)}, bf16[256,640]{1,0:T(8,128)(2,1)S(1)}, u32[]{:S(2)}, u32[]{:S(2)}) %collective-permute-start.9) | collective-permute-done | bytes 327712 | tf_op jit(solution)/shard_map/ppermute | solution.py:211
  47.7 0.1 add_convert_fusion
  47.8 0.8 %fusion = (bf16[128,640]{1,0:T(8,128)(2,1)}, bf16[128,640]{1,0:T(8,128)(2,1)}) fusion(bf16[256,640]{1,0:T(8,128)(2,1)S(1)} %add_convert_fusion), kind=kLoop, calls=%fused_computation.1 | loop fusion | bytes 655360 | tf_op jit(solution)/shard_map/slice | solution.py:304
  (12 shorter events, 0.0 us)
Async XLA Ops:
  0.6 30.8 %copy-start = (bf16[2,4,16,640]{3,2,1,0:T(8,128)(2,1)S(1)}, bf16[2,4,16,640]{3,2,1,0:T(8,128)(2,1)}, u32[]{:S(2)}) copy-start(bf16[2,4,16,640]{3,2,1,0:T(8,128)(2,1)} %param.6) | copy-start | bytes 491524
  0.6 30.8 %copy-start.1 = (bf16[2,4,16,640]{3,2,1,0:T(8,128)(2,1)S(1)}, bf16[2,4,16,640]{3,2,1,0:T(8,128)(2,1)}, u32[]{:S(2)}) copy-start(bf16[2,4,16,640]{3,2,1,0:T(8,128)(2,1)} %param.7) | copy-start | bytes 491524
  0.7 30.8 %copy-start.2 = (bf16[2,4,16,640]{3,2,1,0:T(8,128)(2,1)S(1)}, bf16[2,4,16,640]{3,2,1,0:T(8,128)(2,1)}, u32[]{:S(2)}) copy-start(bf16[2,4,16,640]{3,2,1,0:T(8,128)(2,1)} %param.8) | copy-start | bytes 491524
  0.7 30.8 %copy-start.3 = (bf16[2,4,16,640]{3,2,1,0:T(8,128)(2,1)S(1)}, bf16[2,4,16,640]{3,2,1,0:T(8,128)(2,1)}, u32[]{:S(2)}) copy-start(bf16[2,4,16,640]{3,2,1,0:T(8,128)(2,1)} %param.9) | copy-start | bytes 491524
  3.6 27.8 %copy-start.5 = (s32[8,64]{1,0:T(8,128)S(1)}, s32[8,64]{1,0:T(8,128)}, u32[]{:S(2)}) copy-start(s32[8,64]{1,0:T(8,128)} %refs_13_.1) | copy-start | bytes 6148
  3.6 16.6 %collective-permute-start.2 = (bf16[400,640]{1,0:T(8,128)(2,1)}, bf16[400,640]{1,0:T(8,128)(2,1)S(1)}, u32[]{:S(2)}, u32[]{:S(2)}) collective-permute-start(bf16[400,640]{1,0:T(8,128)(2,1)} %get-tuple-element.13), channel_id=1, source_target_pairs={{0,8},{8,16},{16,24},{24,32},{32,40},{40,48},{48,56},{56,64},{64,7... | collective-permute-start | bytes 1536008 | tf_op jit(solution)/shard_map/ppermute | solution.py:216
  9.0 22.4 %copy-start.4 = (s32[1,2,1,27]{3,2,1,0:T(1,128)S(1)}, s32[1,2,1,27]{3,2,1,0:T(1,128)}, u32[]{:S(2)}) copy-start(s32[1,2,1,27]{3,2,1,0:T(1,128)} %refs_12_.1) | copy-start | bytes 652
  9.0 8.1 %collective-permute-start.1 = (bf16[256,640]{1,0:T(8,128)(2,1)}, bf16[256,640]{1,0:T(8,128)(2,1)S(1)}, u32[]{:S(2)}, u32[]{:S(2)}) collective-permute-start(bf16[256,640]{1,0:T(8,128)(2,1)} %get-tuple-element.12), channel_id=1, source_target_pairs={{128,0},{256,128},{384,256},{129,1},{257,129},{385,257},{130,2},{2... | collective-permute-start | bytes 983048 | tf_op jit(solution)/shard_map/ppermute | solution.py:211
  10.5 9.7 %collective-permute-start = (bf16[256,640]{1,0:T(8,128)(2,1)}, bf16[256,640]{1,0:T(8,128)(2,1)S(1)}, u32[]{:S(2)}, u32[]{:S(2)}) collective-permute-start(bf16[256,640]{1,0:T(8,128)(2,1)} %get-tuple-element.12), channel_id=1, source_target_pairs={{0,128},{128,256},{256,384},{1,129},{129,257},{257,385},{2,130},{1... | collective-permute-start | bytes 983048 | tf_op jit(solution)/shard_map/ppermute | solution.py:211
  14.5 9.9 %collective-permute-start.3 = (bf16[400,640]{1,0:T(8,128)(2,1)}, bf16[400,640]{1,0:T(8,128)(2,1)S(1)}, u32[]{:S(2)}, u32[]{:S(2)}) collective-permute-start(bf16[400,640]{1,0:T(8,128)(2,1)} %get-tuple-element.14), channel_id=1, source_target_pairs={{0,120},{8,0},{16,8},{24,16},{32,24},{40,32},{48,40},{56,48},{64,5... | collective-permute-start | bytes 1536008 | tf_op jit(solution)/shard_map/ppermute | solution.py:216
  17.2 10.7 %collective-permute-start.7 = (bf16[256,640]{1,0:T(8,128)(2,1)S(1)}, bf16[256,640]{1,0:T(8,128)(2,1)S(1)}, u32[]{:S(2)}, u32[]{:S(2)}) collective-permute-start(bf16[256,640]{1,0:T(8,128)(2,1)S(1)} %collective-permute-done.1.refs_5_), channel_id=1, source_target_pairs={{0,120},{8,0},{16,8},{24,16},{32,24},{40,32},{48,40},{56,48},{64,5... | collective-permute-start | bytes 983048 | tf_op jit(solution)/shard_map/ppermute | solution.py:216
  17.2 10.7 %collective-permute-start.5 = (bf16[256,640]{1,0:T(8,128)(2,1)S(1)}, bf16[256,640]{1,0:T(8,128)(2,1)S(1)}, u32[]{:S(2)}, u32[]{:S(2)}) collective-permute-start(bf16[256,640]{1,0:T(8,128)(2,1)S(1)} %collective-permute-done.1.refs_5_), channel_id=1, source_target_pairs={{0,8},{8,16},{16,24},{24,32},{32,40},{40,48},{48,56},{56,64},{64,7... | collective-permute-start | bytes 983048 | tf_op jit(solution)/shard_map/ppermute | solution.py:216
  20.1 11.3 %collective-permute-start.6 = (bf16[256,640]{1,0:T(8,128)(2,1)S(1)}, bf16[256,640]{1,0:T(8,128)(2,1)S(1)}, u32[]{:S(2)}, u32[]{:S(2)}) collective-permute-start(bf16[256,640]{1,0:T(8,128)(2,1)S(1)} %collective-permute-done.refs_4_), channel_id=1, source_target_pairs={{0,120},{8,0},{16,8},{24,16},{32,24},{40,32},{48,40},{56,48},{64,5... | collective-permute-start | bytes 983048 | tf_op jit(solution)/shard_map/ppermute | solution.py:216
  20.2 11.2 %collective-permute-start.4 = (bf16[256,640]{1,0:T(8,128)(2,1)S(1)}, bf16[256,640]{1,0:T(8,128)(2,1)S(1)}, u32[]{:S(2)}, u32[]{:S(2)}) collective-permute-start(bf16[256,640]{1,0:T(8,128)(2,1)S(1)} %collective-permute-done.refs_4_), channel_id=1, source_target_pairs={{0,8},{8,16},{16,24},{24,32},{32,40},{40,48},{48,56},{56,64},{64,7... | collective-permute-start | bytes 983048 | tf_op jit(solution)/shard_map/ppermute | solution.py:216
  36.8 9.2 %collective-permute-start.8 = (bf16[256,640]{1,0:T(8,128)(2,1)S(1)}, bf16[256,640]{1,0:T(8,128)(2,1)S(1)}, u32[]{:S(2)}, u32[]{:S(2)}) collective-permute-start(bf16[256,640]{1,0:T(8,128)(2,1)S(1)} %get-tuple-element.18), channel_id=1, source_target_pairs={{128,0},{256,128},{384,256},{129,1},{257,129},{385,257},{130,2},{2... | collective-permute-start | bytes 983048 | tf_op jit(solution)/shard_map/ppermute | solution.py:211
  38.1 9.6 %collective-permute-start.9 = (bf16[256,640]{1,0:T(8,128)(2,1)S(1)}, bf16[256,640]{1,0:T(8,128)(2,1)S(1)}, u32[]{:S(2)}, u32[]{:S(2)}) collective-permute-start(bf16[256,640]{1,0:T(8,128)(2,1)S(1)} %get-tuple-element.19), channel_id=1, source_target_pairs={{0,128},{128,256},{256,384},{1,129},{129,257},{257,385},{2,130},{1... | collective-permute-start | bytes 983048 | tf_op jit(solution)/shard_map/ppermute | solution.py:211

commit v3 on v2

--- a/solution.py
+++ b/solution.py
@@ -223,35 +223,23 @@
     return held[...]
 
 
-def pack(first, heads, query, key, value, grad, window_mask, pair, near_up, near_down, stage, held, block, sems):
+def pack(first, heads, query, key, value, grad, window_mask, pair, near_up, near_down, held):
     lanes = slice(first * HD, (first + heads) * HD)
-    loads, copies = [], []
-    for part, ref in enumerate((key, value, query, grad)):
-        loads.append(pltpu.make_async_copy(ref.at[:, lanes], stage.at[part], sems.at[part]))
-        loads[-1].start()
-
-    def copy(source, target):
-        copies.append(pltpu.make_async_copy(source, target, sems.at[4 + len(copies)]))
-        copies[-1].start()
-
-    block[...] = padded_masks(window_mask, held).astype(jnp.bfloat16)
+    for part, ref in enumerate((key, value)):
+        rows = slice(part * OWN, (part + 1) * OWN)
+        block = ref[:, lanes]
+        for target in (pair, near_up, near_down):
+            target[rows] = block
+    for part, ref in enumerate((query, grad)):
+        rows = slice(2 * OWN + part * TILE, 2 * OWN + (part + 1) * TILE)
+        block = ref[:, lanes]
+        near_down[rows] = row_tile(block, 0)
+        near_up[rows] = row_tile(block, 1)
+    masks = padded_masks(window_mask, held).astype(jnp.bfloat16)
     rows = slice(2 * OWN + 2 * TILE, 2 * OWN + 2 * TILE + MASK_ROWS)
     for target in (near_up, near_down):
-        copy(block, target.at[rows, :128])
-    for part in range(2):
-        loads[part].wait()
-        rows = slice(part * OWN, (part + 1) * OWN)
-        for target in (pair, near_up, near_down):
-            copy(stage.at[part], target.at[rows])
-    for part in range(2):
-        loads[2 + part].wait()
-        for half, target in enumerate((near_down, near_up)):
-            for frame in range(TF):
-                at = 2 * OWN + part * TILE + frame * HALF
-                start = frame * BAND + half * HALF
-                copy(stage.at[2 + part, start : start + HALF], target.at[at : at + HALF])
-    for started in copies:
-        started.wait()
+        target[rows] = jnp.zeros((MASK_ROWS, heads * HD), jnp.bfloat16)
+        target[rows, :128] = masks
 
 
 def whole():
@@ -270,19 +258,14 @@
                 jax.ShapeDtypeStruct((rows, width), jnp.bfloat16)
                 for rows in (2 * OWN, *[2 * OWN + 2 * TILE + MASK_ROWS] * 2)
             ],
-            in_specs=[pl.BlockSpec(memory_space=pl.ANY)] * 4 + [whole()],
-            out_specs=[pl.BlockSpec(memory_space=pl.ANY)] * 3,
-            scratch_shapes=[
-                pltpu.VMEM((4, OWN, width), jnp.bfloat16),
-                pltpu.VMEM((MASK_ROWS, 128), jnp.float32),
-                pltpu.VMEM((MASK_ROWS, 128), jnp.bfloat16),
-                pltpu.SemaphoreType.DMA((20,)),
-            ],
+            in_specs=[whole()] * 5,
+            out_specs=[whole()] * 3,
+            scratch_shapes=[pltpu.VMEM((MASK_ROWS, 128), jnp.float32)],
             cost_estimate=pl.CostEstimate(flops=0, bytes_accessed=2_000_000, transcendentals=0),
         )(query, key, value, grad, window_mask)
         low, high = shifted(pair, "tm", 1), shifted(pair, "tm", -1)
         above, below = ring(near_up, "row", 1), ring(near_down, "row", -1)
-        far = [jnp.concatenate([low, high])] if LATE == 1 else [low, high]
+        far = [low, high]
         far_above = [ring(x, "row", 1) for x in far]
         far_below = [ring(x, "row", -1) for x in far]
         output, grad_query, own_sum, low_sum, high_sum = pl.pallas_call(

time: 48.8 us -> 48.4 us (level)
  Pallas kernels: 8.24 us -> 7.71 us
    pallas_call x1, Pallas kernels: 2.91 us -> 2.37 us  [shards(): pl.pallas_call(functools.partial(pack, first, heads), out_shape=[jax.Shap...]
where the time goes in v3:
time: 48.4 us; the launch traced here: 48.1 us
  starting transfers between devices  22.1 us (46%)
  waiting for transfers between devices  16.7 us (35%)
  Pallas kernels  7.71 us (16%)
  local copies, waits for them, and re-layouts  0.77 us (2%)
  between operations  0.75 us (2%)
    ppermute x6, starting transfers between devices, ring(): lax.ppermute(value, axis, [(source, (source + steps) % count) for source...  11.3 us
    ppermute x4, starting transfers between devices, shifted(): lax.ppermute(value, axis, [(source, source + steps) for source in range(l...  10.7 us
    ppermute x4, waiting for transfers between devices, shifted(): lax.ppermute(value, axis, [(source, source + steps) for source in range(l...  8.43 us
    ppermute x6, waiting for transfers between devices, ring(): lax.ppermute(value, axis, [(source, (source + steps) % count) for source...  8.3 us
    pallas_call x1, Pallas kernels, shards(): pl.pallas_call(functools.partial(attend, heads, first), out_shape=(jax.Sh...  5.34 us
    pallas_call x1, Pallas kernels, shards(): pl.pallas_call(functools.partial(pack, first, heads), out_shape=[jax.Shap...  2.37 us
  transfers between devices with their start and end apart: 10, of which 6 were waited for; matrix products, arithmetic and copies ran while one was open for 0% of the time, Pallas kernels for 0%

profile of v3, /device:TPU:57, one launch (start us, length us, event | category | flops | bytes accessed | tf_op | source)
XLA Modules:
  0.0 48.1 jit_solution(15050777727240633684)
XLA Ops:
  0.7 2.4 %shard_map.93 = (bf16[256,640]{1,0:T(8,128)(2,1)}, bf16[400,640]{1,0:T(8,128)(2,1)}, bf16[400,640]{1,0:T(8,128)(2,1)}) custom-call(bf16[128,640]{1,0:T(8,128)(2,1)} %bitcast.8, bf16[128,640]{1,0:T(8,128)(2,1)} %bitcast.10, bf16[128,640]{1,0:T(8,128)(2,1)} %bitcast.12, bf16[128,640]{1,0:T(8,128)(2,1)} %bitcast.14, s32[1,2,1,27]{3,2,1,0:T(1,128)} %refs_12_.1), custom_call_target="tpu_custom_call" | custom-call | bytes 2000000 | tf_op jit(solution)/shard_map/pallas_call | solution.py:255
  3.0 5.4 %collective-permute-start.2 = (bf16[400,640]{1,0:T(8,128)(2,1)}, bf16[400,640]{1,0:T(8,128)(2,1)S(1)}, u32[]{:S(2)}, u32[]{:S(2)}) collective-permute-start(bf16[400,640]{1,0:T(8,128)(2,1)} %get-tuple-element.13), channel_id=1, source_target_pairs={{0,8},{8,16},{16,24},{24,32},{32,40},{40,48},{48,56},{56,64},{64,7... | collective-permute-start | bytes 1536008 | tf_op jit(solution)/shard_map/ppermute | solution.py:216
  8.5 1.4 %collective-permute-start.1 = (bf16[256,640]{1,0:T(8,128)(2,1)}, bf16[256,640]{1,0:T(8,128)(2,1)S(1)}, u32[]{:S(2)}, u32[]{:S(2)}) collective-permute-start(bf16[256,640]{1,0:T(8,128)(2,1)} %get-tuple-element.12), channel_id=1, source_target_pairs={{128,0},{256,128},{384,256},{129,1},{257,129},{385,257},{130,2},{2... | collective-permute-start | bytes 983048 | tf_op jit(solution)/shard_map/ppermute | solution.py:211
  9.9 4.0 %collective-permute-start = (bf16[256,640]{1,0:T(8,128)(2,1)}, bf16[256,640]{1,0:T(8,128)(2,1)S(1)}, u32[]{:S(2)}, u32[]{:S(2)}) collective-permute-start(bf16[256,640]{1,0:T(8,128)(2,1)} %get-tuple-element.12), channel_id=1, source_target_pairs={{0,128},{128,256},{256,384},{1,129},{129,257},{257,385},{2,130},{1... | collective-permute-start | bytes 983048 | tf_op jit(solution)/shard_map/ppermute | solution.py:211
  13.9 0.0 collective-permute-start.3
  13.9 2.7 %collective-permute-done.1.refs_5_ = bf16[256,640]{1,0:T(8,128)(2,1)S(1)} collective-permute-done((bf16[256,640]{1,0:T(8,128)(2,1)}, bf16[256,640]{1,0:T(8,128)(2,1)S(1)}, u32[]{:S(2)}, u32[]{:S(2)}) %collective-permute-start.1) | collective-permute-done | bytes 327712 | tf_op jit(solution)/shard_map/ppermute | solution.py:211
  16.6 0.0 collective-permute-start.7
  16.6 3.0 %collective-permute-start.5 = (bf16[256,640]{1,0:T(8,128)(2,1)S(1)}, bf16[256,640]{1,0:T(8,128)(2,1)S(1)}, u32[]{:S(2)}, u32[]{:S(2)}) collective-permute-start(bf16[256,640]{1,0:T(8,128)(2,1)S(1)} %collective-permute-done.1.refs_5_), channel_id=1, source_target_pairs={{0,8},{8,16},{16,24},{24,32},{32,40},{40,48},{48,56},{56,64},{64,7... | collective-permute-start | bytes 983048 | tf_op jit(solution)/shard_map/ppermute | solution.py:216
  19.6 0.0 collective-permute-done.refs_4_
  19.6 0.0 collective-permute-start.6
  19.6 0.0 collective-permute-done.2.refs_6_
  19.6 3.0 %collective-permute-start.4 = (bf16[256,640]{1,0:T(8,128)(2,1)S(1)}, bf16[256,640]{1,0:T(8,128)(2,1)S(1)}, u32[]{:S(2)}, u32[]{:S(2)}) collective-permute-start(bf16[256,640]{1,0:T(8,128)(2,1)S(1)} %collective-permute-done.refs_4_), channel_id=1, source_target_pairs={{0,8},{8,16},{16,24},{24,32},{32,40},{40,48},{48,56},{56,64},{64,7... | collective-permute-start | bytes 983048 | tf_op jit(solution)/shard_map/ppermute | solution.py:216
  22.5 1.3 %collective-permute-done.3.refs_7_ = bf16[400,640]{1,0:T(8,128)(2,1)S(1)} collective-permute-done((bf16[400,640]{1,0:T(8,128)(2,1)}, bf16[400,640]{1,0:T(8,128)(2,1)S(1)}, u32[]{:S(2)}, u32[]{:S(2)}) %collective-permute-start.3) | collective-permute-done | bytes 512032 | tf_op jit(solution)/shard_map/ppermute | solution.py:216
  23.8 3.5 %collective-permute-done.7.refs_11_ = bf16[256,640]{1,0:T(8,128)(2,1)S(1)} collective-permute-done((bf16[256,640]{1,0:T(8,128)(2,1)S(1)}, bf16[256,640]{1,0:T(8,128)(2,1)S(1)}, u32[]{:S(2)}, u32[]{:S(2)}) %collective-permute-start.7) | collective-permute-done | bytes 327712 | tf_op jit(solution)/shard_map/ppermute | solution.py:216
  27.3 0.0 collective-permute-done.5.refs_9_
  27.3 3.5 %collective-permute-done.6.refs_10_ = bf16[256,640]{1,0:T(8,128)(2,1)S(1)} collective-permute-done((bf16[256,640]{1,0:T(8,128)(2,1)S(1)}, bf16[256,640]{1,0:T(8,128)(2,1)S(1)}, u32[]{:S(2)}, u32[]{:S(2)}) %collective-permute-start.6) | collective-permute-done | bytes 327712 | tf_op jit(solution)/shard_map/ppermute | solution.py:216
  30.8 0.0 collective-permute-done.4.refs_8_
  30.9 5.3 %shard_map.94 = (bf16[128,640]{1,0:T(8,128)(2,1)}, bf16[128,640]{1,0:T(8,128)(2,1)}, f32[256,640]{1,0:T(8,128)S(1)}, bf16[256,640]{1,0:T(8,128)(2,1)S(1)}, bf16[256,640]{1,0:T(8,128)(2,1)S(1)}) custom-call(bf16[128,640]{1,0:T(8,128)(2,1)S(1)} %bitcast.9, bf16[128,640]{1,0:T(8,128)(2,1)S(1)} %bitcast.11, bf16[128,640]{1,0:T(8,128)(2,1)S(1)} %bitcast.13, ...), custom_call_target="tpu_custom_call" | custom-call | flops 2000000000 | bytes 8000000 | tf_op jit(solution)/shard_map/pallas_call | solution.py:271
  36.2 1.3 %collective-permute-start.8 = (bf16[256,640]{1,0:T(8,128)(2,1)S(1)}, bf16[256,640]{1,0:T(8,128)(2,1)S(1)}, u32[]{:S(2)}, u32[]{:S(2)}) collective-permute-start(bf16[256,640]{1,0:T(8,128)(2,1)S(1)} %get-tuple-element.18), channel_id=1, source_target_pairs={{128,0},{256,128},{384,256},{129,1},{257,129},{385,257},{130,2},{2... | collective-permute-start | bytes 983048 | tf_op jit(solution)/shard_map/ppermute | solution.py:211
  37.5 4.0 %collective-permute-start.9 = (bf16[256,640]{1,0:T(8,128)(2,1)S(1)}, bf16[256,640]{1,0:T(8,128)(2,1)S(1)}, u32[]{:S(2)}, u32[]{:S(2)}) collective-permute-start(bf16[256,640]{1,0:T(8,128)(2,1)S(1)} %get-tuple-element.19), channel_id=1, source_target_pairs={{0,128},{128,256},{256,384},{1,129},{129,257},{257,385},{2,130},{1... | collective-permute-start | bytes 983048 | tf_op jit(solution)/shard_map/ppermute | solution.py:211
  41.5 4.0 %collective-permute-done.8 = bf16[256,640]{1,0:T(8,128)(2,1)S(1)} collective-permute-done((bf16[256,640]{1,0:T(8,128)(2,1)S(1)}, bf16[256,640]{1,0:T(8,128)(2,1)S(1)}, u32[]{:S(2)}, u32[]{:S(2)}) %collective-permute-start.8) | collective-permute-done | bytes 327712 | tf_op jit(solution)/shard_map/ppermute | solution.py:211
  45.5 1.8 %collective-permute-done.9 = bf16[256,640]{1,0:T(8,128)(2,1)S(1)} collective-permute-done((bf16[256,640]{1,0:T(8,128)(2,1)S(1)}, bf16[256,640]{1,0:T(8,128)(2,1)S(1)}, u32[]{:S(2)}, u32[]{:S(2)}) %collective-permute-start.9) | collective-permute-done | bytes 327712 | tf_op jit(solution)/shard_map/ppermute | solution.py:211
  47.3 0.1 add_convert_fusion
  47.4 0.8 %fusion = (bf16[128,640]{1,0:T(8,128)(2,1)}, bf16[128,640]{1,0:T(8,128)(2,1)}) fusion(bf16[256,640]{1,0:T(8,128)(2,1)S(1)} %add_convert_fusion), kind=kLoop, calls=%fused_computation.1 | loop fusion | bytes 655360 | tf_op jit(solution)/shard_map/slice | solution.py:287
  (12 shorter events, 0.0 us)
Async XLA Ops:
  0.6 30.2 %copy-start = (bf16[2,4,16,640]{3,2,1,0:T(8,128)(2,1)S(1)}, bf16[2,4,16,640]{3,2,1,0:T(8,128)(2,1)}, u32[]{:S(2)}) copy-start(bf16[2,4,16,640]{3,2,1,0:T(8,128)(2,1)} %param.6) | copy-start | bytes 491524
  0.6 30.2 %copy-start.1 = (bf16[2,4,16,640]{3,2,1,0:T(8,128)(2,1)S(1)}, bf16[2,4,16,640]{3,2,1,0:T(8,128)(2,1)}, u32[]{:S(2)}) copy-start(bf16[2,4,16,640]{3,2,1,0:T(8,128)(2,1)} %param.7) | copy-start | bytes 491524
  0.7 30.2 %copy-start.2 = (bf16[2,4,16,640]{3,2,1,0:T(8,128)(2,1)S(1)}, bf16[2,4,16,640]{3,2,1,0:T(8,128)(2,1)}, u32[]{:S(2)}) copy-start(bf16[2,4,16,640]{3,2,1,0:T(8,128)(2,1)} %param.8) | copy-start | bytes 491524
  0.7 30.2 %copy-start.3 = (bf16[2,4,16,640]{3,2,1,0:T(8,128)(2,1)S(1)}, bf16[2,4,16,640]{3,2,1,0:T(8,128)(2,1)}, u32[]{:S(2)}) copy-start(bf16[2,4,16,640]{3,2,1,0:T(8,128)(2,1)} %param.9) | copy-start | bytes 491524
  3.0 27.8 %copy-start.5 = (s32[8,64]{1,0:T(8,128)S(1)}, s32[8,64]{1,0:T(8,128)}, u32[]{:S(2)}) copy-start(s32[8,64]{1,0:T(8,128)} %refs_13_.1) | copy-start | bytes 6148
  3.0 16.5 %collective-permute-start.2 = (bf16[400,640]{1,0:T(8,128)(2,1)}, bf16[400,640]{1,0:T(8,128)(2,1)S(1)}, u32[]{:S(2)}, u32[]{:S(2)}) collective-permute-start(bf16[400,640]{1,0:T(8,128)(2,1)} %get-tuple-element.13), channel_id=1, source_target_pairs={{0,8},{8,16},{16,24},{24,32},{32,40},{40,48},{48,56},{56,64},{64,7... | collective-permute-start | bytes 1536008 | tf_op jit(solution)/shard_map/ppermute | solution.py:216
  8.5 22.4 %copy-start.4 = (s32[1,2,1,27]{3,2,1,0:T(1,128)S(1)}, s32[1,2,1,27]{3,2,1,0:T(1,128)}, u32[]{:S(2)}) copy-start(s32[1,2,1,27]{3,2,1,0:T(1,128)} %refs_12_.1) | copy-start | bytes 652
  8.5 8.1 %collective-permute-start.1 = (bf16[256,640]{1,0:T(8,128)(2,1)}, bf16[256,640]{1,0:T(8,128)(2,1)S(1)}, u32[]{:S(2)}, u32[]{:S(2)}) collective-permute-start(bf16[256,640]{1,0:T(8,128)(2,1)} %get-tuple-element.12), channel_id=1, source_target_pairs={{128,0},{256,128},{384,256},{129,1},{257,129},{385,257},{130,2},{2... | collective-permute-start | bytes 983048 | tf_op jit(solution)/shard_map/ppermute | solution.py:211
  9.9 9.7 %collective-permute-start = (bf16[256,640]{1,0:T(8,128)(2,1)}, bf16[256,640]{1,0:T(8,128)(2,1)S(1)}, u32[]{:S(2)}, u32[]{:S(2)}) collective-permute-start(bf16[256,640]{1,0:T(8,128)(2,1)} %get-tuple-element.12), channel_id=1, source_target_pairs={{0,128},{128,256},{256,384},{1,129},{129,257},{257,385},{2,130},{1... | collective-permute-start | bytes 983048 | tf_op jit(solution)/shard_map/ppermute | solution.py:211
  13.9 9.9 %collective-permute-start.3 = (bf16[400,640]{1,0:T(8,128)(2,1)}, bf16[400,640]{1,0:T(8,128)(2,1)S(1)}, u32[]{:S(2)}, u32[]{:S(2)}) collective-permute-start(bf16[400,640]{1,0:T(8,128)(2,1)} %get-tuple-element.14), channel_id=1, source_target_pairs={{0,120},{8,0},{16,8},{24,16},{32,24},{40,32},{48,40},{56,48},{64,5... | collective-permute-start | bytes 1536008 | tf_op jit(solution)/shard_map/ppermute | solution.py:216
  16.6 10.7 %collective-permute-start.7 = (bf16[256,640]{1,0:T(8,128)(2,1)S(1)}, bf16[256,640]{1,0:T(8,128)(2,1)S(1)}, u32[]{:S(2)}, u32[]{:S(2)}) collective-permute-start(bf16[256,640]{1,0:T(8,128)(2,1)S(1)} %collective-permute-done.1.refs_5_), channel_id=1, source_target_pairs={{0,120},{8,0},{16,8},{24,16},{32,24},{40,32},{48,40},{56,48},{64,5... | collective-permute-start | bytes 983048 | tf_op jit(solution)/shard_map/ppermute | solution.py:216
  16.6 10.7 %collective-permute-start.5 = (bf16[256,640]{1,0:T(8,128)(2,1)S(1)}, bf16[256,640]{1,0:T(8,128)(2,1)S(1)}, u32[]{:S(2)}, u32[]{:S(2)}) collective-permute-start(bf16[256,640]{1,0:T(8,128)(2,1)S(1)} %collective-permute-done.1.refs_5_), channel_id=1, source_target_pairs={{0,8},{8,16},{16,24},{24,32},{32,40},{40,48},{48,56},{56,64},{64,7... | collective-permute-start | bytes 983048 | tf_op jit(solution)/shard_map/ppermute | solution.py:216
  19.6 11.3 %collective-permute-start.6 = (bf16[256,640]{1,0:T(8,128)(2,1)S(1)}, bf16[256,640]{1,0:T(8,128)(2,1)S(1)}, u32[]{:S(2)}, u32[]{:S(2)}) collective-permute-start(bf16[256,640]{1,0:T(8,128)(2,1)S(1)} %collective-permute-done.refs_4_), channel_id=1, source_target_pairs={{0,120},{8,0},{16,8},{24,16},{32,24},{40,32},{48,40},{56,48},{64,5... | collective-permute-start | bytes 983048 | tf_op jit(solution)/shard_map/ppermute | solution.py:216
  19.6 11.2 %collective-permute-start.4 = (bf16[256,640]{1,0:T(8,128)(2,1)S(1)}, bf16[256,640]{1,0:T(8,128)(2,1)S(1)}, u32[]{:S(2)}, u32[]{:S(2)}) collective-permute-start(bf16[256,640]{1,0:T(8,128)(2,1)S(1)} %collective-permute-done.refs_4_), channel_id=1, source_target_pairs={{0,8},{8,16},{16,24},{24,32},{32,40},{40,48},{48,56},{56,64},{64,7... | collective-permute-start | bytes 983048 | tf_op jit(solution)/shard_map/ppermute | solution.py:216
  36.2 9.3 %collective-permute-start.8 = (bf16[256,640]{1,0:T(8,128)(2,1)S(1)}, bf16[256,640]{1,0:T(8,128)(2,1)S(1)}, u32[]{:S(2)}, u32[]{:S(2)}) collective-permute-start(bf16[256,640]{1,0:T(8,128)(2,1)S(1)} %get-tuple-element.18), channel_id=1, source_target_pairs={{128,0},{256,128},{384,256},{129,1},{257,129},{385,257},{130,2},{2... | collective-permute-start | bytes 983048 | tf_op jit(solution)/shard_map/ppermute | solution.py:211
  37.5 9.8 %collective-permute-start.9 = (bf16[256,640]{1,0:T(8,128)(2,1)S(1)}, bf16[256,640]{1,0:T(8,128)(2,1)S(1)}, u32[]{:S(2)}, u32[]{:S(2)}) collective-permute-start(bf16[256,640]{1,0:T(8,128)(2,1)S(1)} %get-tuple-element.19), channel_id=1, source_target_pairs={{0,128},{128,256},{256,384},{1,129},{129,257},{257,385},{2,130},{1... | collective-permute-start | bytes 983048 | tf_op jit(solution)/shard_map/ppermute | solution.py:211

commit v4 on v3

--- a/solution.py
+++ b/solution.py
@@ -98,18 +98,18 @@
 
 
 def attend(heads, first, *refs):
-    (query_ref, key_ref, value_ref, grad_ref, low, high, above, below), refs = refs[:8], refs[8:]
+    (query_ref, key_ref, value_ref, grad_ref, low, high, above, below, query_above, query_below), refs = refs[:10], refs[10:]
     far_above, far_below, refs = refs[:LATE], refs[LATE : 2 * LATE], refs[2 * LATE :]
     (window_mask, row_valid), refs = refs[:2], refs[2:]
     output, grad_query, own_sum, low_sum, high_sum, held = refs
 
-    mask_at = 2 * OWN + 2 * TILE
+    mask_at = 2 * TILE
     here, up, down = (
         block.astype(jnp.float32)
         for block in (
             padded_masks(window_mask, held),
-            above[mask_at : mask_at + MASK_ROWS, :128],
-            below[mask_at : mask_at + MASK_ROWS, :128],
+            query_above[mask_at : mask_at + MASK_ROWS, :128],
+            query_below[mask_at : mask_at + MASK_ROWS, :128],
         )
     )
     sources = (here[0:1], here[1:2], up[1:2], down[0:1])
@@ -143,14 +143,11 @@
         lanes = slice(head * HD, (head + 1) * HD)
         arg_lanes = slice((first + head) * HD, (first + head + 1) * HD)
         query_own, grad_own = query_ref[:, arg_lanes], grad_ref[:, arg_lanes]
-        at = 2 * OWN
-        query = jnp.concatenate(
-            [row_tile(query_own, 0), row_tile(query_own, 1), above[at : at + TILE, lanes], below[at : at + TILE, lanes]]
-        )
-        at += TILE
-        grad = jnp.concatenate(
-            [row_tile(grad_own, 0), row_tile(grad_own, 1), above[at : at + TILE, lanes], below[at : at + TILE, lanes]]
-        )
+        query = [row_tile(query_own, 0), row_tile(query_own, 1), query_above[:TILE, lanes], query_below[:TILE, lanes]]
+        query = jnp.concatenate(query)
+        near = slice(TILE, 2 * TILE)
+        grad = [row_tile(grad_own, 0), row_tile(grad_own, 1), query_above[near, lanes], query_below[near, lanes]]
+        grad = jnp.concatenate(grad)
 
         def region(part, ref):
             rows = slice(part * OWN, (part + 1) * OWN)
@@ -223,23 +220,14 @@
     return held[...]
 
 
-def pack(first, heads, query, key, value, grad, window_mask, pair, near_up, near_down, held):
+def pack(first, heads, query, grad, window_mask, up, down, held):
     lanes = slice(first * HD, (first + heads) * HD)
-    for part, ref in enumerate((key, value)):
-        rows = slice(part * OWN, (part + 1) * OWN)
-        block = ref[:, lanes]
-        for target in (pair, near_up, near_down):
-            target[rows] = block
-    for part, ref in enumerate((query, grad)):
-        rows = slice(2 * OWN + part * TILE, 2 * OWN + (part + 1) * TILE)
-        block = ref[:, lanes]
-        near_down[rows] = row_tile(block, 0)
-        near_up[rows] = row_tile(block, 1)
     masks = padded_masks(window_mask, held).astype(jnp.bfloat16)
-    rows = slice(2 * OWN + 2 * TILE, 2 * OWN + 2 * TILE + MASK_ROWS)
-    for target in (near_up, near_down):
-        target[rows] = jnp.zeros((MASK_ROWS, heads * HD), jnp.bfloat16)
-        target[rows, :128] = masks
+    for half, message in enumerate((down, up)):
+        message[:TILE] = row_tile(query[:, lanes], half)
+        message[TILE : 2 * TILE] = row_tile(grad[:, lanes], half)
+        message[2 * TILE :] = jnp.zeros((MASK_ROWS, heads * HD), jnp.bfloat16)
+        message[2 * TILE :, :128] = masks
 
 
 def whole():
@@ -252,20 +240,21 @@
     parts = []
     for first, heads in GROUPS:
         width = heads * HD
-        pair, near_up, near_down = pl.pallas_call(
+        lanes = slice(first * HD, (first + heads) * HD)
+        pair = jnp.concatenate([key[:, lanes], value[:, lanes]])
+        low, high = shifted(pair, "tm", 1), shifted(pair, "tm", -1)
+        above, below = ring(pair, "row", 1), ring(pair, "row", -1)
+        up, down = pl.pallas_call(
             functools.partial(pack, first, heads),
-            out_shape=[
-                jax.ShapeDtypeStruct((rows, width), jnp.bfloat16)
-                for rows in (2 * OWN, *[2 * OWN + 2 * TILE + MASK_ROWS] * 2)
-            ],
-            in_specs=[whole()] * 5,
-            out_specs=[whole()] * 3,
+            out_shape=[jax.ShapeDtypeStruct((2 * TILE + MASK_ROWS, width), jnp.bfloat16)] * 2,
+            in_specs=[whole()] * 3,
+            out_specs=[whole()] * 2,
             scratch_shapes=[pltpu.VMEM((MASK_ROWS, 128), jnp.float32)],
-            cost_estimate=pl.CostEstimate(flops=0, bytes_accessed=2_000_000, transcendentals=0),
-        )(query, key, value, grad, window_mask)
-        low, high = shifted(pair, "tm", 1), shifted(pair, "tm", -1)
-        above, below = ring(near_up, "row", 1), ring(near_down, "row", -1)
-        far = [low, high]
+            cost_estimate=pl.CostEstimate(flops=0, bytes_accessed=700_000, transcendentals=0),
+        )(query, grad, window_mask)
+        up, down, high = lax.optimization_barrier((up, down, high))
+        query_above, query_below = ring(up, "row", 1), ring(down, "row", -1)
+        far = [jnp.concatenate([low, high])] if LATE == 1 else [low, high]
         far_above = [ring(x, "row", 1) for x in far]
         far_below = [ring(x, "row", -1) for x in far]
         output, grad_query, own_sum, low_sum, high_sum = pl.pallas_call(
@@ -277,12 +266,12 @@
                 jax.ShapeDtypeStruct((2 * OWN, width), jnp.bfloat16),
                 jax.ShapeDtypeStruct((2 * OWN, width), jnp.bfloat16),
             ),
-            in_specs=[whole()] * (10 + 2 * LATE),
+            in_specs=[whole()] * (12 + 2 * LATE),
             out_specs=(whole(),) * 5,
             scratch_shapes=[pltpu.VMEM((MASK_ROWS, 128), jnp.float32)],
             compiler_params=pltpu.CompilerParams(vmem_limit_bytes=40 * 1024 * 1024),
             cost_estimate=pl.CostEstimate(flops=heads * 400_000_000, bytes_accessed=8_000_000, transcendentals=0),
-        )(query, key, value, grad, low, high, above, below, *far_above, *far_below, window_mask, row_valid)
+        )(query, key, value, grad, low, high, above, below, query_above, query_below, *far_above, *far_below, window_mask, row_valid)
         total = own_sum + shifted(low_sum, "tm", -1).astype(jnp.float32) + shifted(high_sum, "tm", 1).astype(jnp.float32)
         parts.append((output, grad_query, total[:OWN].astype(jnp.bfloat16), total[OWN:].astype(jnp.bfloat16)))
     return tuple(jnp.concatenate(pieces, axis=1).reshape(queries.shape) for pieces in zip(*parts))

time: 48.4 us -> 47.6 us (0.983); the launches traced: 48.1 us -> 46.7 us
  starting transfers between devices: 22.1 us -> 20.8 us
  other arithmetic: 0.13 us -> 1.19 us
  waiting for transfers between devices: 16.7 us -> 16 us
  Pallas kernels: 7.71 us -> 7.1 us
    ppermute x4, waiting for transfers between devices: 8.43 us -> 5.82 us  [shifted(): lax.ppermute(value, axis, [(source, source + steps) for source in range(l...]
    ppermute x6 -> x8, waiting for transfers between devices: 8.3 us -> 10.2 us  [ring(): lax.ppermute(value, axis, [(source, (source + steps) % count) for source...]
    ppermute x6 -> x8, starting transfers between devices: 11.3 us -> 9.62 us  [ring(): lax.ppermute(value, axis, [(source, (source + steps) % count) for source...]
    concatenate x0 -> x1, other arithmetic: none -> 1.07 us  [shards(): pair = jnp.concatenate([key[:, lanes], value[:, lanes]])]
    pallas_call x1, Pallas kernels: 2.37 us -> 1.79 us  [shards(): pl.pallas_call(functools.partial(pack, first, heads), out_shape=[jax.Shap...]
    ppermute x4, starting transfers between devices: 10.7 us -> 11.2 us  [shifted(): lax.ppermute(value, axis, [(source, source + steps) for source in range(l...]
  transfers between devices with their start and end apart: 10 -> 12, of which waited for: 6 -> 4; matrix products, arithmetic and copies ran while one was open for 0% -> 0% of each run, Pallas kernels for 0% -> 4%
where the time goes in v4:
time: 47.6 us; the launch traced here: 46.7 us
  starting transfers between devices  20.8 us (44%)
  waiting for transfers between devices  16 us (34%)
  Pallas kernels  7.1 us (15%)
  other arithmetic  1.19 us (2%)
  local copies, waits for them, and re-layouts  0.78 us (2%)
  between operations  0.76 us (2%)
    ppermute x4, starting transfers between devices, shifted(): lax.ppermute(value, axis, [(source, source + steps) for source in range(l...  11.2 us
    ppermute x8, waiting for transfers between devices, ring(): lax.ppermute(value, axis, [(source, (source + steps) % count) for source...  10.2 us
    ppermute x8, starting transfers between devices, ring(): lax.ppermute(value, axis, [(source, (source + steps) % count) for source...  9.62 us
    ppermute x4, waiting for transfers between devices, shifted(): lax.ppermute(value, axis, [(source, source + steps) for source in range(l...  5.82 us
    pallas_call x1, Pallas kernels, shards(): pl.pallas_call(functools.partial(attend, heads, first), out_shape=(jax.Sh...  5.31 us
    pallas_call x1, Pallas kernels, shards(): pl.pallas_call(functools.partial(pack, first, heads), out_shape=[jax.Shap...  1.79 us
    concatenate x1, other arithmetic, shards(): pair = jnp.concatenate([key[:, lanes], value[:, lanes]])  1.07 us
  transfers between devices with their start and end apart: 12, of which 4 were waited for; matrix products, arithmetic and copies ran while one was open for 0% of the time, Pallas kernels for 4%

profile of v4, /device:TPU:57, one launch (start us, length us, event | category | flops | bytes accessed | tf_op | source)
XLA Modules:
  0.0 46.7 jit_solution(10180100135166227779)
XLA Ops:
  0.6 0.0 copy-start.2
  0.6 0.0 copy-start.3
  0.7 1.1 %pad_maximum_fusion = bf16[256,640]{1,0:T(8,128)(2,1)S(1)} fusion(bf16[128,640]{1,0:T(8,128)(2,1)} %bitcast.10, bf16[128,640]{1,0:T(8,128)(2,1)} %bitcast.8), kind=kLoop, calls=%fused_computation.1 | loop fusion | flops 655360 | bytes 655360 | tf_op jit(solution)/shard_map/concatenate | solution.py:244
  1.7 1.3 %collective-permute-start.1 = (bf16[256,640]{1,0:T(8,128)(2,1)S(1)}, bf16[256,640]{1,0:T(8,128)(2,1)S(1)}, u32[]{:S(2)}, u32[]{:S(2)}) collective-permute-start(bf16[256,640]{1,0:T(8,128)(2,1)S(1)} %pad_maximum_fusion), channel_id=1, source_target_pairs={{128,0},{256,128},{384,256},{129,1},{257,129},{385,257},{130,2},{2... | collective-permute-start | bytes 983048 | tf_op jit(solution)/shard_map/ppermute | solution.py:208
  3.0 4.6 %collective-permute-start = (bf16[256,640]{1,0:T(8,128)(2,1)S(1)}, bf16[256,640]{1,0:T(8,128)(2,1)S(1)}, u32[]{:S(2)}, u32[]{:S(2)}) collective-permute-start(bf16[256,640]{1,0:T(8,128)(2,1)S(1)} %pad_maximum_fusion), channel_id=1, source_target_pairs={{0,128},{128,256},{256,384},{1,129},{129,257},{257,385},{2,130},{1... | collective-permute-start | bytes 983048 | tf_op jit(solution)/shard_map/ppermute | solution.py:208
  7.7 1.0 %collective-permute-start.3 = (bf16[256,640]{1,0:T(8,128)(2,1)S(1)}, bf16[256,640]{1,0:T(8,128)(2,1)S(1)}, u32[]{:S(2)}, u32[]{:S(2)}) collective-permute-start(bf16[256,640]{1,0:T(8,128)(2,1)S(1)} %pad_maximum_fusion), channel_id=1, source_target_pairs={{0,120},{8,0},{16,8},{24,16},{32,24},{40,32},{48,40},{56,48},{64,5... | collective-permute-start | bytes 983048 | tf_op jit(solution)/shard_map/ppermute | solution.py:213
  8.7 4.4 %collective-permute-start.2 = (bf16[256,640]{1,0:T(8,128)(2,1)S(1)}, bf16[256,640]{1,0:T(8,128)(2,1)S(1)}, u32[]{:S(2)}, u32[]{:S(2)}) collective-permute-start(bf16[256,640]{1,0:T(8,128)(2,1)S(1)} %pad_maximum_fusion), channel_id=1, source_target_pairs={{0,8},{8,16},{16,24},{24,32},{32,40},{40,48},{48,56},{56,64},{64,7... | collective-permute-start | bytes 983048 | tf_op jit(solution)/shard_map/ppermute | solution.py:213
  13.1 1.8 %shard_map.93 = (bf16[144,640]{1,0:T(8,128)(2,1)}, bf16[144,640]{1,0:T(8,128)(2,1)}) custom-call(bf16[128,640]{1,0:T(8,128)(2,1)} %bitcast.12, bf16[128,640]{1,0:T(8,128)(2,1)} %bitcast.14, s32[1,2,1,27]{3,2,1,0:T(1,128)} %refs_14_.1), custom_call_target="tpu_custom_call" | custom-call | bytes 700000 | tf_op jit(solution)/shard_map/pallas_call | solution.py:247
  14.9 0.0 collective-permute-done.1.refs_5_
  14.9 1.3 %collective-permute-start.4 = (bf16[144,640]{1,0:T(8,128)(2,1)}, bf16[144,640]{1,0:T(8,128)(2,1)S(1)}, u32[]{:S(2)}, u32[]{:S(2)}) collective-permute-start(bf16[144,640]{1,0:T(8,128)(2,1)} %get-tuple-element.17), channel_id=1, source_target_pairs={{0,8},{8,16},{16,24},{24,32},{32,40},{40,48},{48,56},{56,64},{64,7... | collective-permute-start | bytes 552968 | tf_op jit(solution)/shard_map/ppermute | solution.py:213
  16.1 0.0 collective-permute-start.9
  16.1 0.0 collective-permute-start.8
  16.2 1.7 %collective-permute-done.3.refs_7_ = bf16[256,640]{1,0:T(8,128)(2,1)S(1)} collective-permute-done((bf16[256,640]{1,0:T(8,128)(2,1)S(1)}, bf16[256,640]{1,0:T(8,128)(2,1)S(1)}, u32[]{:S(2)}, u32[]{:S(2)}) %collective-permute-start.3) | collective-permute-done | bytes 327712 | tf_op jit(solution)/shard_map/ppermute | solution.py:213
  17.8 1.3 %collective-permute-start.6 = (bf16[256,640]{1,0:T(8,128)(2,1)S(1)}, bf16[256,640]{1,0:T(8,128)(2,1)S(1)}, u32[]{:S(2)}, u32[]{:S(2)}) collective-permute-start(bf16[256,640]{1,0:T(8,128)(2,1)S(1)} %collective-permute-done.refs_4_), channel_id=1, source_target_pairs={{0,8},{8,16},{16,24},{24,32},{32,40},{40,48},{48,56},{56,64},{64,7... | collective-permute-start | bytes 983048 | tf_op jit(solution)/shard_map/ppermute | solution.py:213
  19.1 1.7 %collective-permute-start.7 = (bf16[256,640]{1,0:T(8,128)(2,1)S(1)}, bf16[256,640]{1,0:T(8,128)(2,1)S(1)}, u32[]{:S(2)}, u32[]{:S(2)}) collective-permute-start(bf16[256,640]{1,0:T(8,128)(2,1)S(1)} %collective-permute-done.1.refs_5_), channel_id=1, source_target_pairs={{0,8},{8,16},{16,24},{24,32},{32,40},{40,48},{48,56},{56,64},{64,7... | collective-permute-start | bytes 983048 | tf_op jit(solution)/shard_map/ppermute | solution.py:213
  20.8 0.0 collective-permute-done.4.refs_8_
  20.8 8.5 %collective-permute-done.5.refs_9_ = bf16[144,640]{1,0:T(8,128)(2,1)S(1)} collective-permute-done((bf16[144,640]{1,0:T(8,128)(2,1)}, bf16[144,640]{1,0:T(8,128)(2,1)S(1)}, u32[]{:S(2)}, u32[]{:S(2)}) %collective-permute-start.5) | collective-permute-done | bytes 184352 | tf_op jit(solution)/shard_map/ppermute | solution.py:213
  29.4 5.3 %shard_map.94 = (bf16[128,640]{1,0:T(8,128)(2,1)}, bf16[128,640]{1,0:T(8,128)(2,1)}, f32[256,640]{1,0:T(8,128)S(1)}, bf16[256,640]{1,0:T(8,128)(2,1)S(1)}, bf16[256,640]{1,0:T(8,128)(2,1)S(1)}) custom-call(bf16[128,640]{1,0:T(8,128)(2,1)S(1)} %bitcast.13, bf16[128,640]{1,0:T(8,128)(2,1)S(1)} %bitcast.9, bf16[128,640]{1,0:T(8,128)(2,1)S(1)} %bitcast.11, ...), custom_call_target="tpu_custom_call" | custom-call | flops 2000000000 | bytes 8000000 | tf_op jit(solution)/shard_map/pallas_call | solution.py:260
  34.7 1.3 %collective-permute-start.10 = (bf16[256,640]{1,0:T(8,128)(2,1)S(1)}, bf16[256,640]{1,0:T(8,128)(2,1)S(1)}, u32[]{:S(2)}, u32[]{:S(2)}) collective-permute-start(bf16[256,640]{1,0:T(8,128)(2,1)S(1)} %get-tuple-element.22), channel_id=1, source_target_pairs={{128,0},{256,128},{384,256},{129,1},{257,129},{385,257},{130,2},{2... | collective-permute-start | bytes 983048 | tf_op jit(solution)/shard_map/ppermute | solution.py:208
  36.0 4.0 %collective-permute-start.11 = (bf16[256,640]{1,0:T(8,128)(2,1)S(1)}, bf16[256,640]{1,0:T(8,128)(2,1)S(1)}, u32[]{:S(2)}, u32[]{:S(2)}) collective-permute-start(bf16[256,640]{1,0:T(8,128)(2,1)S(1)} %get-tuple-element.23), channel_id=1, source_target_pairs={{0,128},{128,256},{256,384},{1,129},{129,257},{257,385},{2,130},{1... | collective-permute-start | bytes 983048 | tf_op jit(solution)/shard_map/ppermute | solution.py:208
  40.0 4.1 %collective-permute-done.10 = bf16[256,640]{1,0:T(8,128)(2,1)S(1)} collective-permute-done((bf16[256,640]{1,0:T(8,128)(2,1)S(1)}, bf16[256,640]{1,0:T(8,128)(2,1)S(1)}, u32[]{:S(2)}, u32[]{:S(2)}) %collective-permute-start.10) | collective-permute-done | bytes 327712 | tf_op jit(solution)/shard_map/ppermute | solution.py:208
  44.1 1.8 %collective-permute-done.11 = bf16[256,640]{1,0:T(8,128)(2,1)S(1)} collective-permute-done((bf16[256,640]{1,0:T(8,128)(2,1)S(1)}, bf16[256,640]{1,0:T(8,128)(2,1)S(1)}, u32[]{:S(2)}, u32[]{:S(2)}) %collective-permute-start.11) | collective-permute-done | bytes 327712 | tf_op jit(solution)/shard_map/ppermute | solution.py:208
  45.8 0.1 add_convert_fusion
  46.0 0.8 %fusion = (bf16[128,640]{1,0:T(8,128)(2,1)}, bf16[128,640]{1,0:T(8,128)(2,1)}) fusion(bf16[256,640]{1,0:T(8,128)(2,1)S(1)} %add_convert_fusion), kind=kLoop, calls=%fused_computation.2 | loop fusion | bytes 655360 | tf_op jit(solution)/shard_map/slice | solution.py:276
  (17 shorter events, 0.0 us)
Async XLA Ops:
  0.6 28.7 %copy-start.2 = (bf16[2,4,16,640]{3,2,1,0:T(8,128)(2,1)S(1)}, bf16[2,4,16,640]{3,2,1,0:T(8,128)(2,1)}, u32[]{:S(2)}) copy-start(bf16[2,4,16,640]{3,2,1,0:T(8,128)(2,1)} %param.6) | copy-start | bytes 491524
  0.6 28.7 %copy-start.3 = (bf16[2,4,16,640]{3,2,1,0:T(8,128)(2,1)S(1)}, bf16[2,4,16,640]{3,2,1,0:T(8,128)(2,1)}, u32[]{:S(2)}) copy-start(bf16[2,4,16,640]{3,2,1,0:T(8,128)(2,1)} %param.9) | copy-start | bytes 491524
  0.7 28.7 %copy-start.5 = (s32[8,64]{1,0:T(8,128)S(1)}, s32[8,64]{1,0:T(8,128)}, u32[]{:S(2)}) copy-start(s32[8,64]{1,0:T(8,128)} %refs_15_.1) | copy-start | bytes 6148
  1.7 13.1 %collective-permute-start.1 = (bf16[256,640]{1,0:T(8,128)(2,1)S(1)}, bf16[256,640]{1,0:T(8,128)(2,1)S(1)}, u32[]{:S(2)}, u32[]{:S(2)}) collective-permute-start(bf16[256,640]{1,0:T(8,128)(2,1)S(1)} %pad_maximum_fusion), channel_id=1, source_target_pairs={{128,0},{256,128},{384,256},{129,1},{257,129},{385,257},{130,2},{2... | collective-permute-start | bytes 983048 | tf_op jit(solution)/shard_map/ppermute | solution.py:208
  3.0 13.1 %collective-permute-start = (bf16[256,640]{1,0:T(8,128)(2,1)S(1)}, bf16[256,640]{1,0:T(8,128)(2,1)S(1)}, u32[]{:S(2)}, u32[]{:S(2)}) collective-permute-start(bf16[256,640]{1,0:T(8,128)(2,1)S(1)} %pad_maximum_fusion), channel_id=1, source_target_pairs={{0,128},{128,256},{256,384},{1,129},{129,257},{257,385},{2,130},{1... | collective-permute-start | bytes 983048 | tf_op jit(solution)/shard_map/ppermute | solution.py:208
  7.7 10.1 %collective-permute-start.3 = (bf16[256,640]{1,0:T(8,128)(2,1)S(1)}, bf16[256,640]{1,0:T(8,128)(2,1)S(1)}, u32[]{:S(2)}, u32[]{:S(2)}) collective-permute-start(bf16[256,640]{1,0:T(8,128)(2,1)S(1)} %pad_maximum_fusion), channel_id=1, source_target_pairs={{0,120},{8,0},{16,8},{24,16},{32,24},{40,32},{48,40},{56,48},{64,5... | collective-permute-start | bytes 983048 | tf_op jit(solution)/shard_map/ppermute | solution.py:213
  8.7 10.5 %collective-permute-start.2 = (bf16[256,640]{1,0:T(8,128)(2,1)S(1)}, bf16[256,640]{1,0:T(8,128)(2,1)S(1)}, u32[]{:S(2)}, u32[]{:S(2)}) collective-permute-start(bf16[256,640]{1,0:T(8,128)(2,1)S(1)} %pad_maximum_fusion), channel_id=1, source_target_pairs={{0,8},{8,16},{16,24},{24,32},{32,40},{40,48},{48,56},{56,64},{64,7... | collective-permute-start | bytes 983048 | tf_op jit(solution)/shard_map/ppermute | solution.py:213
  13.1 16.3 %copy-start = (bf16[2,4,16,640]{3,2,1,0:T(8,128)(2,1)S(1)}, bf16[2,4,16,640]{3,2,1,0:T(8,128)(2,1)}, u32[]{:S(2)}) copy-start(bf16[2,4,16,640]{3,2,1,0:T(8,128)(2,1)} %param.7) | copy-start | bytes 491524
  13.1 16.3 %copy-start.1 = (bf16[2,4,16,640]{3,2,1,0:T(8,128)(2,1)S(1)}, bf16[2,4,16,640]{3,2,1,0:T(8,128)(2,1)}, u32[]{:S(2)}) copy-start(bf16[2,4,16,640]{3,2,1,0:T(8,128)(2,1)} %param.8) | copy-start | bytes 491524
  14.9 14.5 %copy-start.4 = (s32[1,2,1,27]{3,2,1,0:T(1,128)S(1)}, s32[1,2,1,27]{3,2,1,0:T(1,128)}, u32[]{:S(2)}) copy-start(s32[1,2,1,27]{3,2,1,0:T(1,128)} %refs_14_.1) | copy-start | bytes 652
  14.9 5.9 %collective-permute-start.4 = (bf16[144,640]{1,0:T(8,128)(2,1)}, bf16[144,640]{1,0:T(8,128)(2,1)S(1)}, u32[]{:S(2)}, u32[]{:S(2)}) collective-permute-start(bf16[144,640]{1,0:T(8,128)(2,1)} %get-tuple-element.17), channel_id=1, source_target_pairs={{0,8},{8,16},{16,24},{24,32},{32,40},{40,48},{48,56},{56,64},{64,7... | collective-permute-start | bytes 552968 | tf_op jit(solution)/shard_map/ppermute | solution.py:213
  16.1 13.2 %collective-permute-start.9 = (bf16[256,640]{1,0:T(8,128)(2,1)S(1)}, bf16[256,640]{1,0:T(8,128)(2,1)S(1)}, u32[]{:S(2)}, u32[]{:S(2)}) collective-permute-start(bf16[256,640]{1,0:T(8,128)(2,1)S(1)} %collective-permute-done.1.refs_5_), channel_id=1, source_target_pairs={{0,120},{8,0},{16,8},{24,16},{32,24},{40,32},{48,40},{56,48},{64,5... | collective-permute-start | bytes 983048 | tf_op jit(solution)/shard_map/ppermute | solution.py:213
  16.1 13.2 %collective-permute-start.8 = (bf16[256,640]{1,0:T(8,128)(2,1)S(1)}, bf16[256,640]{1,0:T(8,128)(2,1)S(1)}, u32[]{:S(2)}, u32[]{:S(2)}) collective-permute-start(bf16[256,640]{1,0:T(8,128)(2,1)S(1)} %collective-permute-done.refs_4_), channel_id=1, source_target_pairs={{0,120},{8,0},{16,8},{24,16},{32,24},{40,32},{48,40},{56,48},{64,5... | collective-permute-start | bytes 983048 | tf_op jit(solution)/shard_map/ppermute | solution.py:213
  17.8 11.5 %collective-permute-start.6 = (bf16[256,640]{1,0:T(8,128)(2,1)S(1)}, bf16[256,640]{1,0:T(8,128)(2,1)S(1)}, u32[]{:S(2)}, u32[]{:S(2)}) collective-permute-start(bf16[256,640]{1,0:T(8,128)(2,1)S(1)} %collective-permute-done.refs_4_), channel_id=1, source_target_pairs={{0,8},{8,16},{16,24},{24,32},{32,40},{40,48},{48,56},{56,64},{64,7... | collective-permute-start | bytes 983048 | tf_op jit(solution)/shard_map/ppermute | solution.py:213
  19.1 10.2 %collective-permute-start.7 = (bf16[256,640]{1,0:T(8,128)(2,1)S(1)}, bf16[256,640]{1,0:T(8,128)(2,1)S(1)}, u32[]{:S(2)}, u32[]{:S(2)}) collective-permute-start(bf16[256,640]{1,0:T(8,128)(2,1)S(1)} %collective-permute-done.1.refs_5_), channel_id=1, source_target_pairs={{0,8},{8,16},{16,24},{24,32},{32,40},{40,48},{48,56},{56,64},{64,7... | collective-permute-start | bytes 983048 | tf_op jit(solution)/shard_map/ppermute | solution.py:213
  20.8 8.5 %collective-permute-start.5 = (bf16[144,640]{1,0:T(8,128)(2,1)}, bf16[144,640]{1,0:T(8,128)(2,1)S(1)}, u32[]{:S(2)}, u32[]{:S(2)}) collective-permute-start(bf16[144,640]{1,0:T(8,128)(2,1)} %get-tuple-element.18), channel_id=1, source_target_pairs={{0,120},{8,0},{16,8},{24,16},{32,24},{40,32},{48,40},{56,48},{64,5... | collective-permute-start | bytes 552968 | tf_op jit(solution)/shard_map/ppermute | solution.py:213
  34.7 9.4 %collective-permute-start.10 = (bf16[256,640]{1,0:T(8,128)(2,1)S(1)}, bf16[256,640]{1,0:T(8,128)(2,1)S(1)}, u32[]{:S(2)}, u32[]{:S(2)}) collective-permute-start(bf16[256,640]{1,0:T(8,128)(2,1)S(1)} %get-tuple-element.22), channel_id=1, source_target_pairs={{128,0},{256,128},{384,256},{129,1},{257,129},{385,257},{130,2},{2... | collective-permute-start | bytes 983048 | tf_op jit(solution)/shard_map/ppermute | solution.py:208
  36.0 9.8 %collective-permute-start.11 = (bf16[256,640]{1,0:T(8,128)(2,1)S(1)}, bf16[256,640]{1,0:T(8,128)(2,1)S(1)}, u32[]{:S(2)}, u32[]{:S(2)}) collective-permute-start(bf16[256,640]{1,0:T(8,128)(2,1)S(1)} %get-tuple-element.23), channel_id=1, source_target_pairs={{0,128},{128,256},{256,384},{1,129},{129,257},{257,385},{2,130},{1... | collective-permute-start | bytes 983048 | tf_op jit(solution)/shard_map/ppermute | solution.py:208
